TPU v7x, 256 devices: a whole 4x4x8 slice. The times are simulated.
256 devices in a mesh: seq: 32 (over y, z), dp: 8 (over x, core).
Axes of the slice: x: 4, y: 4, z: 8, core: 2. Of those that a mesh axis runs over, the one named last changes fastest.
Arguments:
- inputs: bfloat16 [8, 4096, 2048], P('dp', 'seq'), may hold values from -6 to 6
- query_rows: bfloat16 [8, 4096, 2048], P('dp', 'seq'), may hold values from -6 to 6
- key_rows: bfloat16 [8, 4096, 2048], P('dp', 'seq'), may hold values from -6 to 6
- cotangent: bfloat16 [8, 4096, 2048], P('dp', 'seq'), may hold values from -6 to 6
- w_value: bfloat16 [2048, 2048], P('seq'), may hold values from -0.125 to 0.125
Outputs:
- grad_query: bfloat16 [8, 4096, 2048], P('dp', 'seq')
- grad_key: bfloat16 [8, 4096, 2048], P('dp', 'seq')
- grad_weight: float32 [2048, 2048], P('seq')
All inputs are finite; a program needn't handle non-finite values.
Results may differ from a plain program's by a relative error of at most 0.025.
Values may be sent and summed in bfloat16 or wider, within the bound.
No kernel may reach another device: no remote copies, remote signals or barrier semaphores. Data moves between devices by JAX's collectives and lax.ppermute only.
A program may use at most 192 MiB of HBM per device.

v0:
```python
import math

import jax
import jax.numpy as jnp
from jax import lax
from jax.sharding import PartitionSpec as P

HEAD = 128


def carried_in(part, axis, combine, identity, reverse):
    count = lax.axis_size(axis)
    place = lax.axis_index(axis)
    ahead = count - 1 - place if reverse else place
    gathered = lax.all_gather(part, axis)
    state = jnp.zeros_like(part) + jnp.asarray(identity, part.dtype)

    def one(step, state):
        source = count - 1 - step if reverse else step
        return combine(state, lax.dynamic_index_in_dim(gathered, source, 0, False))

    return lax.fori_loop(0, ahead, one, state)


def add_single(earlier, later):
    return earlier + later


def on_device(inputs, query_rows, key_rows, cotangent, w_value):
    batch_dev, rows, width = inputs.shape
    width_all = query_rows.shape[2]
    heads = width_all // HEAD
    length = rows * lax.axis_size("seq")
    scale = 1.0 / math.sqrt(HEAD * length)
    grad_scale = 1.0 / math.sqrt(batch_dev * lax.axis_size("dp") * length)
    flat_inputs = inputs.reshape(batch_dev * rows, width)
    columns = flat_inputs
    values = jnp.dot(
        columns,
        lax.all_gather(w_value, "seq", axis=0, tiled=True),
        preferred_element_type=jnp.float32,
    ).astype(jnp.bfloat16)

    def split_heads(array_in):
        return array_in.reshape(batch_dev, rows, heads, HEAD)

    q_heads = split_heads(query_rows)
    k_heads = split_heads(key_rows)
    v_heads = split_heads(values)
    g_heads = split_heads(cotangent)
    kv_local = jnp.einsum("bthd,bthe->bhde", k_heads, v_heads, preferred_element_type=jnp.float32)
    qg_local = jnp.einsum("bthd,bthe->bhde", q_heads, g_heads, preferred_element_type=jnp.float32)
    zero_state = jnp.zeros_like(kv_local)
    kv_before = carried_in(kv_local, "seq", add_single, zero_state, False)
    qg_after = carried_in(qg_local, "seq", add_single, zero_state, True)
    kv_round = kv_before.astype(jnp.bfloat16)
    qg_round = qg_after.astype(jnp.bfloat16)
    positions = jnp.arange(rows, dtype=jnp.int32)
    causal = positions[:, None] >= positions[None, :]
    score_gv = (
        jnp.einsum("bthd,bshd->bhts", g_heads, v_heads, preferred_element_type=jnp.float32) * scale
    )
    score_gv = jnp.where(causal[None, None], score_gv, 0.0).astype(jnp.bfloat16)
    score_qk = (
        jnp.einsum("bthd,bshd->bhts", q_heads, k_heads, preferred_element_type=jnp.float32) * scale
    )
    score_qk = jnp.where(causal[None, None], score_qk, 0.0).astype(jnp.bfloat16)
    grad_q = scale * jnp.einsum(
        "bthe,bhde->bthd", g_heads, kv_round, preferred_element_type=jnp.float32
    )
    grad_q = grad_q + jnp.einsum(
        "bhts,bshd->bthd", score_gv, k_heads, preferred_element_type=jnp.float32
    )
    grad_k = scale * jnp.einsum(
        "bshe,bhde->bshd", v_heads, qg_round, preferred_element_type=jnp.float32
    )
    grad_k = grad_k + jnp.einsum(
        "bhts,bthd->bshd", score_gv, q_heads, preferred_element_type=jnp.float32
    )
    grad_v = scale * jnp.einsum(
        "bshd,bhde->bshe", k_heads, qg_round, preferred_element_type=jnp.float32
    )
    grad_v = grad_v + jnp.einsum(
        "bhts,bthe->bshe", score_qk, g_heads, preferred_element_type=jnp.float32
    )
    grad_query = grad_q.astype(jnp.bfloat16).reshape(batch_dev, rows, width_all)
    grad_key = grad_k.astype(jnp.bfloat16).reshape(batch_dev, rows, width_all)
    flat_grad_values = grad_v.astype(jnp.bfloat16).reshape(batch_dev * rows, width_all)
    columns = flat_inputs
    product = lax.dot_general(
        columns, flat_grad_values, (((0,), (0,)), ((), ())), preferred_element_type=jnp.float32
    )
    partial_grad = lax.psum_scatter(
        (product * grad_scale).astype(jnp.bfloat16), "seq", scatter_dimension=0, tiled=True
    )
    grad_weight = lax.psum(partial_grad, "dp").astype(jnp.float32)
    return (grad_query, grad_key, grad_weight)


def solution(mesh):
    placed = (
        P("dp", "seq", None),
        P("dp", "seq", None),
        P("dp", "seq", None),
        P("dp", "seq", None),
        P("seq", None),
    )
    return jax.shard_map(
        on_device,
        mesh=mesh,
        in_specs=placed,
        out_specs=(P("dp", "seq", None), P("dp", "seq", None), P("seq", None)),
        check_vma=False,
    )
```

profile of v0, /device:TPU:1, one launch (start us, length us, event | category | flops | bytes accessed | tf_op | source)
XLA Modules:
  0.0 881.9 jit_solution(5524947250726285007)
XLA Ops:
  10.4 1.5 fusion.31
  13.2 99.3 %all-gather.6.cloned.1.call-done = bf16[2048,2048]{1,0:T(8,128)(2,1)} async-done(((bf16[64,2048]{1,0:T(8,128)(2,1)}), bf16[2048,2048]{1,0:T(8,128)(2,1)}) %all-gather.6.cloned.1.call-update) | async-done | bytes 8388624 | tf_op jit(solution)/shard_map/all_gather | solution.py:40
  112.5 4.6 fusion.12
  121.0 224.6 %all-gather.10.cloned.1.call-done = f32[512,128,128]{2,1,0:T(8,128)} async-done(((f32[16,128,128]{2,1,0:T(8,128)}), f32[512,128,128]{2,1,0:T(8,128)}) %all-gather.10.cloned.1.call-update) | async-done | bytes 33554448 | tf_op jit(solution)/shard_map/all_gather | solution.py:15
  345.7 47.4 %while.23 = (s32[]{:T(128)}, f32[1,16,128,128]{3,2,1,0:T(8,128)S(1)}, s32[]{:T(128)}, f32[32,1,16,128,128]{4,3,2,1,0:T(8,128)}, s32[]{:T(128)}, /*index=5*/s32[]{:T(128)}, s32[]{:T(128)}, s32[]{:T(128)}) while((s32[]{:T(128)}, f32[1,16,128,128]{3,2,1,0:T(8,128)S(1)}, s32[]{:T(128)}, f32[32,1,16,128,128]{4,3,2,1,0:T(8,128)}, s32[]{:T(128)}, ...), condition=%wide.region_3.4_spmd, body=%wide.region_2.3_spmd.sunk | while | flops 262150 | bytes 3145863 | solution.py:22
  357.8 1.6 bitcast_add_fusion.5
  359.5 1.5 bitcast_add_fusion.5
  365.6 1.5 bitcast_add_fusion.5
  367.2 1.5 bitcast_add_fusion.5
  368.7 1.5 bitcast_add_fusion.5
  379.4 1.5 bitcast_add_fusion.5
  380.9 1.5 bitcast_add_fusion.5
  382.5 1.5 bitcast_add_fusion.5
  384.0 1.5 bitcast_add_fusion.5
  385.5 1.5 bitcast_add_fusion.5
  394.6 2.6 fusion.11
  397.3 6.6 fusion
  403.9 12.5 %copy.52 = bf16[2048,2048]{1,0:T(8,128)(2,1)} copy(bf16[2048,2048]{0,1:T(8,128)(2,1)} %fusion) | data formatting | bytes 16777216
  418.9 159.7 %all-gather.8.cloned.1.call-done = f32[512,128,128]{2,1,0:T(8,128)} async-done(((f32[16,128,128]{2,1,0:T(8,128)}), f32[512,128,128]{2,1,0:T(8,128)}) %all-gather.8.cloned.1.call-update) | async-done | bytes 33554448 | tf_op jit(solution)/shard_map/all_gather | solution.py:15
  580.0 225.1 %reduce-scatter.4.cloned.1.call-done = bf16[64,2048]{1,0:T(8,128)(2,1)} async-done(((bf16[2048,2048]{1,0:T(8,128)(2,1)}), bf16[64,2048]{1,0:T(8,128)(2,1)}) %reduce-scatter.4.cloned.1.call-update) | async-done | bytes 262160
  805.1 2.0 copy.53
  807.1 1.7 fusion.9
  809.8 63.5 %all-reduce.2.cloned.1.call-done = bf16[64,2048]{0,1:T(8,128)(2,1)} async-done(((bf16[64,2048]{0,1:T(8,128)(2,1)}), bf16[64,2048]{0,1:T(8,128)(2,1)}) %all-reduce.2.cloned.1.call-update) | async-done | bytes 262160 | tf_op jit(solution)/shard_map/psum | solution.py:96
  873.4 2.0 copy.48
  (60 shorter events, 45.9 us)
Async XLA Ops:
  7.2 105.4 %copy-start = (bf16[1,128,2048]{2,1,0:T(8,128)(2,1)S(1)}, bf16[1,128,2048]{2,1,0:T(8,128)(2,1)}, u32[]{:S(2)}) copy-start(bf16[1,128,2048]{2,1,0:T(8,128)(2,1)} %param.9) | copy-start | bytes 1572868
  7.2 105.4 %all-gather.6.cloned.1.call-start = ((), (), s32[]{:S(2)}) async-start(), calls=%async_computation.1 | async-start | bytes 8650752 | tf_op jit(solution)/shard_map/all_gather | solution.py:40
  7.9 337.6 %all-gather.10.cloned.1.call-start = ((), (), s32[]{:S(2)}) async-start(), calls=%async_computation.4 | async-start | bytes 34603008 | tf_op jit(solution)/shard_map/all_gather | solution.py:15
  12.0 566.6 %all-gather.8.cloned.1.call-start = ((), (), s32[]{:S(2)}) async-start(), calls=%async_computation.3 | async-start | bytes 34603008 | tf_op jit(solution)/shard_map/all_gather | solution.py:15
  117.2 0.8 copy-start.1
  119.7 685.4 %reduce-scatter.4.cloned.1.call-start = ((), (), s32[]{:S(2)}) async-start(), calls=%async_computation.5 | async-start | bytes 8650752
  397.3 19.2 %copy-start.2 = (bf16[16,16,8,128]{3,2,1,0:T(8,128)(2,1)S(1)}, bf16[16,16,8,128]{3,2,1,0:T(8,128)(2,1)}, u32[]{:S(2)}) copy-start(bf16[16,16,8,128]{3,2,1,0:T(8,128)(2,1)} %copy-done.1) | copy-start | bytes 1572868
  416.4 456.9 %all-reduce.2.cloned.1.call-start = ((), (), s32[]{:S(2)}) async-start(), calls=%async_computation.2 | async-start | bytes 1048576 | tf_op jit(solution)/shard_map/psum | solution.py:96
  417.0 0.9 copy-start.4
  417.5 389.6 %copy-start.3 = (bf16[128,16,128]{0,2,1:T(8,128)(2,1)S(1)}, bf16[128,16,128]{0,2,1:T(8,128)(2,1)}, u32[]{:S(2)}) copy-start(bf16[128,16,128]{0,2,1:T(8,128)(2,1)} %copy.37) | copy-start | bytes 1572868
  417.9 389.2 %copy-start.5 = (bf16[16,128,128]{2,1,0:T(8,128)(2,1)S(1)}, bf16[16,128,128]{2,1,0:T(8,128)(2,1)}, u32[]{:S(2)}) copy-start(bf16[16,128,128]{2,1,0:T(8,128)(2,1)} %copy-done.4) | copy-start | bytes 1572868
Sparse Core Ops, SparseCore 0:
  10.6 101.8 all-gather.5
  115.1 230.3 all-gather.9
  348.2 230.3 all-gather.7
  582.4 222.5 reduce-scatter.3
  807.4 65.9 all-reduce.1
where the time goes:
time: 885 us; the launch traced here: 882 us
  waiting for transfers between devices  773 us (87%)
  other arithmetic  46.6 us (5%)
  local copies, waits for them, and re-layouts  25.6 us (3%)
  matrix products  21.6 us (2%)
  between operations  13.9 us (2%)
    all_gather x2, waiting for transfers between devices, carried_in(): gathered = lax.all_gather(part, axis)  384 us
    unnamed x6, waiting for transfers between devices  226 us
    all_gather x1, waiting for transfers between devices, on_device(): lax.all_gather(w_value, 'seq', axis=0, tiled=True)  99.3 us
    psum x1, waiting for transfers between devices, on_device(): grad_weight = lax.psum(partial_grad, 'dp').astype(jnp.float32)  63.5 us
    add x31, other arithmetic, add_single(): return earlier + later  46.6 us
    unnamed x19, local copies, waits for them, and re-layouts  21.6 us
  transfers between devices with their start and end apart: 5, of which 5 were waited for; matrix products, arithmetic and copies ran while one was open for 10% of the time, Pallas kernels for 0%

commit v1 on v0

v1 whole, which is shorter than its diff:
```python
import functools
import math

import jax
import jax.numpy as jnp
from jax import lax
from jax.experimental import pallas as pl
from jax.experimental.pallas import tpu as pltpu
from jax.sharding import PartitionSpec as P

HEAD = 128
F32 = jnp.float32
BF16 = jnp.bfloat16


def dot(a, b, a_dim, b_dim):
    return lax.dot_general(a, b, (((a_dim,), (b_dim,)), ((), ())), preferred_element_type=F32)


def cols(h):
    return slice(h * HEAD, (h + 1) * HEAD)


def state_kernel(left_ref, right_ref, out_ref):
    for h in range(left_ref.shape[1] // HEAD):
        out_ref[cols(h), :] = dot(left_ref[:, cols(h)], right_ref[:, cols(h)], 0, 0).astype(BF16)


def block_state_kernel(left_ref, right_ref, out_ref):
    per = right_ref.shape[2] // HEAD
    for h in range(left_ref.shape[1] // HEAD):
        right = right_ref[h // per, :, cols(h % per)]
        out_ref[cols(h), :] = dot(left_ref[:, cols(h)], right, 0, 0).astype(BF16)


def prefix_kernel(reverse, part_ref, out_ref):
    count = part_ref.shape[0]
    total = jnp.zeros(part_ref.shape[1:], F32)
    for step in range(count):
        i = count - 1 - step if reverse else step
        out_ref[i] = total.astype(BF16)
        total = total + part_ref[i].astype(F32)


def causal_mask(rows):
    t = lax.broadcasted_iota(jnp.int32, (rows, rows), 0)
    s = lax.broadcasted_iota(jnp.int32, (rows, rows), 1)
    return t >= s


def grad_values_kernel(scale, q_ref, k_ref, g_ref, qg_ref, out_ref):
    mask = causal_mask(q_ref.shape[0])
    per = out_ref.shape[2] // HEAD
    for h in range(q_ref.shape[1] // HEAD):
        q, k, g = q_ref[:, cols(h)], k_ref[:, cols(h)], g_ref[:, cols(h)]
        score = jnp.where(mask, dot(q, k, 1, 1) * scale, 0.0).astype(BF16)
        grad = scale * dot(k, qg_ref[cols(h), :], 1, 0) + dot(score, g, 0, 0)
        out_ref[h // per, :, cols(h % per)] = grad.astype(BF16)


def grad_rows_kernel(scale, q_ref, k_ref, g_ref, v_ref, kv_ref, qg_ref, gq_ref, gk_ref):
    mask = causal_mask(q_ref.shape[0])
    per = v_ref.shape[2] // HEAD
    for h in range(q_ref.shape[1] // HEAD):
        q, k, g = q_ref[:, cols(h)], k_ref[:, cols(h)], g_ref[:, cols(h)]
        v = v_ref[h // per, :, cols(h % per)]
        score = jnp.where(mask, dot(g, v, 1, 1) * scale, 0.0).astype(BF16)
        grad_q = scale * dot(g, kv_ref[cols(h), :], 1, 1) + dot(score, k, 1, 0)
        gq_ref[:, cols(h)] = grad_q.astype(BF16)
        grad_k = scale * dot(v, qg_ref[cols(h), :], 1, 1) + dot(score, q, 0, 0)
        gk_ref[:, cols(h)] = grad_k.astype(BF16)


def reduce_kernel(factor, part_ref, out_ref):
    total = part_ref[0].astype(F32)
    for i in range(1, part_ref.shape[0]):
        total = total + part_ref[i].astype(F32)
    out_ref[...] = total * factor


def call(kernel, shapes, flops, *operands):
    out = [jax.ShapeDtypeStruct(s, d) for s, d in shapes]
    moved = sum(x.size * x.dtype.itemsize for x in list(operands) + out)
    result = pl.pallas_call(
        kernel,
        out_shape=out,
        in_specs=[pl.BlockSpec(memory_space=pltpu.VMEM)] * len(operands),
        out_specs=[pl.BlockSpec(memory_space=pltpu.VMEM)] * len(out),
        compiler_params=pltpu.CompilerParams(vmem_limit_bytes=24 * 2**20),
        cost_estimate=pl.CostEstimate(flops=flops, bytes_accessed=moved, transcendentals=0),
    )(*operands)
    return result[0] if len(result) == 1 else result


def on_device(inputs, query_rows, key_rows, cotangent, w_value):
    rows, width = inputs.shape[1:]
    width_all = query_rows.shape[2]
    heads = width_all // HEAD
    seq, dp = lax.axis_size("seq"), lax.axis_size("dp")
    scale = 1.0 / math.sqrt(HEAD * rows * seq)
    grad_scale = 1.0 / math.sqrt(inputs.shape[0] * dp * rows * seq)
    block = width_all // dp
    q, k, g = query_rows[0], key_rows[0], cotangent[0]
    head_flops = 2 * rows * HEAD * HEAD * heads

    def exchange(array, axis):
        return lax.all_to_all(array, axis, 0, 0, tiled=True)

    def carried(state, reverse):
        parts = exchange(state.reshape(seq, -1, HEAD), "seq")
        sums = call(
            functools.partial(prefix_kernel, reverse), [(parts.shape, BF16)], parts.size, parts
        )
        return exchange(sums, "seq").reshape(state.shape)

    all_inputs = lax.all_gather(inputs, "dp", axis=0, tiled=True).reshape(dp * rows, width)
    own = lax.dynamic_slice_in_dim(w_value, lax.axis_index("dp") * block, block, 1)
    columns = exchange(jnp.broadcast_to(own[None], (seq,) + own.shape), "seq").reshape(width, block)

    qg_local = call(state_kernel, [((heads * HEAD, HEAD), BF16)], head_flops, q, g)
    qg_round = carried(qg_local, True)

    values = jnp.dot(all_inputs, columns, preferred_element_type=F32).astype(BF16)
    values = exchange(values.reshape(dp, rows, block), "dp")
    kv_local = call(block_state_kernel, [((heads * HEAD, HEAD), BF16)], head_flops, k, values)
    kv_round = carried(kv_local, False)

    grad_values = call(
        functools.partial(grad_values_kernel, scale),
        [((dp, rows, block), BF16)], 3 * head_flops, q, k, g, qg_round,
    )
    grad_values = exchange(grad_values, "dp").reshape(dp * rows, block)
    product = dot(all_inputs, grad_values, 0, 0).astype(BF16)
    parts = exchange(product.reshape(seq, width // seq, block), "seq")
    summed = call(
        functools.partial(reduce_kernel, grad_scale), [(parts.shape[1:], F32)], parts.size, parts
    )
    grad_weight = lax.all_gather(summed, "dp", axis=1, tiled=True)

    grad_query, grad_key = call(
        functools.partial(grad_rows_kernel, scale),
        [((rows, width_all), BF16)] * 2, 5 * head_flops, q, k, g, values, kv_round, qg_round,
    )
    return grad_query[None], grad_key[None], grad_weight


def solution(mesh):
    placed = (
        P("dp", "seq", None),
        P("dp", "seq", None),
        P("dp", "seq", None),
        P("dp", "seq", None),
        P("seq", None),
    )
    return jax.shard_map(
        on_device,
        mesh=mesh,
        in_specs=placed,
        out_specs=(P("dp", "seq", None), P("dp", "seq", None), P("seq", None)),
        check_vma=False,
    )
```

time: 885 us -> 217 us (0.25)
  waiting for transfers between devices: 773 us -> 94.5 us
  starting transfers between devices: 0.2 us -> 62.5 us
  other arithmetic: 46.6 us -> 0 us
  local copies, waits for them, and re-layouts: 25.6 us -> 9.99 us
  blocking collectives: 0 us -> 15.5 us
  matrix products: 21.6 us -> 8.56 us
  Pallas kernels: 0 us -> 10.7 us
    all_gather x3 -> x1, waiting for transfers between devices: 484 us -> 0.02 us  [on_device(): lax.all_gather(inputs, 'dp', axis=0, tiled=True).reshape(dp * rows, width)]
    unnamed x6 -> x1, waiting for transfers between devices: 226 us -> 0.68 us
    all_to_all x0 -> x8, waiting for transfers between devices: none -> 93.8 us  [exchange(): return lax.all_to_all(array, axis, 0, 0, tiled=True)]
    psum x1 -> x0, waiting for transfers between devices: 63.5 us -> none  [on_device(): grad_weight = lax.psum(partial_grad, 'dp').astype(jnp.float32)]
    all_to_all x0 -> x8, starting transfers between devices: none -> 62.5 us  [exchange(): return lax.all_to_all(array, axis, 0, 0, tiled=True)]
    add x31 -> x0, other arithmetic: 46.6 us -> none  [add_single(): return earlier + later]
    unnamed x19, local copies, waits for them, and re-layouts: 21.6 us -> 5.56 us
    all_gather x0 -> x1, blocking collectives: none -> 15.5 us  [on_device(): grad_weight = lax.all_gather(summed, 'dp', axis=1, tiled=True)]
  transfers between devices with their start and end apart: 5 -> 9, of which waited for: 5 -> 7; matrix products, arithmetic and copies ran while one was open for 10% -> 6% of each run, Pallas kernels for 0% -> 3%
where the time goes in v1:
time: 217 us; the launch traced here: 216 us
  waiting for transfers between devices  94.5 us (44%)
  starting transfers between devices  62.5 us (29%)
  blocking collectives  15.5 us (7%)
  between operations  14.2 us (7%)
  Pallas kernels  10.7 us (5%)
  local copies, waits for them, and re-layouts  9.99 us (5%)
  matrix products  8.56 us (4%)
    all_to_all x8, waiting for transfers between devices, exchange(): return lax.all_to_all(array, axis, 0, 0, tiled=True)  93.8 us
    all_to_all x8, starting transfers between devices, exchange(): return lax.all_to_all(array, axis, 0, 0, tiled=True)  62.5 us
    all_gather x1, blocking collectives, on_device(): grad_weight = lax.all_gather(summed, 'dp', axis=1, tiled=True)  15.5 us
    pallas_call x7, Pallas kernels, call(): pl.pallas_call(kernel, out_shape=out, in_specs=[pl.BlockSpec(memory_space...  10.7 us
    unnamed x19, local copies, waits for them, and re-layouts  5.56 us
    dot_general x1, matrix products, dot(): lax.dot_general(a, b, (((a_dim,), (b_dim,)), ((), ())), preferred_element...  4.64 us
  transfers between devices with their start and end apart: 9, of which 7 were waited for; matrix products, arithmetic and copies ran while one was open for 6% of the time, Pallas kernels for 3%

profile of v1, /device:TPU:1, one launch (start us, length us, event | category | flops | bytes accessed | tf_op | source)
XLA Modules:
  0.0 216.0 jit_solution(9117479605955712562)
XLA Ops:
  11.1 12.0 %all-to-all-start.4 = ((bf16[32,64,128]{2,1,0:T(8,128)(2,1)}), bf16[32,64,128]{2,1,0:T(8,128)(2,1)S(1)}, u32[]{:S(2)}, u32[]{:S(2)}) async-start(bf16[32,64,128]{2,1,0:T(8,128)(2,1)} %bitcast.9), calls=%async_computation.4 | async-start | bytes 1048576 | tf_op jit(solution)/shard_map/all_to_all | solution.py:107
  23.2 14.3 %all-to-all-done.4.part_ref = bf16[32,64,128]{2,1,0:T(8,128)(2,1)S(1)} async-done(((bf16[32,64,128]{2,1,0:T(8,128)(2,1)}), bf16[32,64,128]{2,1,0:T(8,128)(2,1)S(1)}, u32[]{:S(2)}, u32[]{:S(2)}) %all-to-all-start.4) | async-done | bytes 524320 | tf_op jit(solution)/shard_map/all_to_all | solution.py:107
  38.6 7.5 %all-to-all-start = ((bf16[32,64,256]{2,1,0:T(8,128)(2,1)}), bf16[32,64,256]{2,1,0:T(8,128)(2,1)S(1)}, u32[]{:S(2)}, u32[]{:S(2)}) async-start(bf16[32,64,256]{2,1,0:T(8,128)(2,1)} %broadcast_in_dim.12), calls=%async_computation | async-start | bytes 2097152 | tf_op jit(solution)/shard_map/all_to_all | solution.py:107
  47.0 23.8 %all-to-all-done = bf16[32,64,256]{2,1,0:T(8,128)(2,1)S(1)} async-done(((bf16[32,64,256]{2,1,0:T(8,128)(2,1)}), bf16[32,64,256]{2,1,0:T(8,128)(2,1)S(1)}, u32[]{:S(2)}, u32[]{:S(2)}) %all-to-all-start) | async-done | bytes 1048608 | tf_op jit(solution)/shard_map/all_to_all | solution.py:107
  70.8 8.6 %all-to-all-start.5 = ((bf16[32,64,128]{2,1,0:T(8,128)(2,1)}), bf16[32,64,128]{2,1,0:T(8,128)(2,1)S(1)}, u32[]{:S(2)}, u32[]{:S(2)}) async-start(bf16[32,64,128]{2,1,0:T(8,128)(2,1)} %shard_map.79), calls=%async_computation.5 | async-start | bytes 1048576 | tf_op jit(solution)/shard_map/all_to_all | solution.py:107
  79.4 3.9 %fusion.2 = bf16[1024,256]{0,1:T(8,128)(2,1)S(1)} fusion(bf16[2048,256]{1,0:T(8,128)(2,1)} %bitcast.41, bf16[1024,2048]{1,0:T(8,128)(2,1)} %bitcast.39), kind=kOutput, calls=%fused_computation.4 | convolution fusion | flops 1074003968 | bytes 5767168 | tf_op jit(solution)/shard_map/dot_general | solution.py:123
  84.3 8.7 %all-to-all-done.5 = bf16[32,64,128]{2,1,0:T(8,128)(2,1)S(1)} async-done(((bf16[32,64,128]{2,1,0:T(8,128)(2,1)}), bf16[32,64,128]{2,1,0:T(8,128)(2,1)S(1)}, u32[]{:S(2)}, u32[]{:S(2)}) %all-to-all-start.5) | async-done | bytes 524320 | tf_op jit(solution)/shard_map/all_to_all | solution.py:107
  93.1 8.8 %all-to-all-start.1 = ((bf16[8,128,256]{2,1,0:T(8,128)(2,1)}), bf16[8,128,256]{2,1,0:T(8,128)(2,1)S(1)}, u32[]{:S(2)}, u32[]{:S(2)}) async-start(bf16[8,128,256]{2,1,0:T(8,128)(2,1)} %bitcast.6), calls=%async_computation.1 | async-start | bytes 1048576 | tf_op jit(solution)/shard_map/all_to_all | solution.py:107
  101.9 1.7 shard_map.81
  103.7 7.7 %all-to-all-done.1.right_ref.v_ref = bf16[8,128,256]{2,1,0:T(8,128)(2,1)S(1)} async-done(((bf16[8,128,256]{2,1,0:T(8,128)(2,1)}), bf16[8,128,256]{2,1,0:T(8,128)(2,1)S(1)}, u32[]{:S(2)}, u32[]{:S(2)}) %all-to-all-start.1) | async-done | bytes 524320 | tf_op jit(solution)/shard_map/all_to_all | solution.py:107
  111.4 4.3 %all-to-all-start.6 = ((bf16[8,128,256]{2,1,0:T(8,128)(2,1)}), bf16[8,128,256]{2,1,0:T(8,128)(2,1)S(1)}, u32[]{:S(2)}, u32[]{:S(2)}) async-start(bf16[8,128,256]{2,1,0:T(8,128)(2,1)} %shard_map.81), calls=%async_computation.6 | async-start | bytes 1048576 | tf_op jit(solution)/shard_map/all_to_all | solution.py:107
  115.7 1.1 shard_map.76
  116.8 8.4 %all-to-all-done.6 = bf16[8,128,256]{2,1,0:T(8,128)(2,1)S(1)} async-done(((bf16[8,128,256]{2,1,0:T(8,128)(2,1)}), bf16[8,128,256]{2,1,0:T(8,128)(2,1)S(1)}, u32[]{:S(2)}, u32[]{:S(2)}) %all-to-all-start.6) | async-done | bytes 524320 | tf_op jit(solution)/shard_map/all_to_all | solution.py:107
  126.0 4.9 %all-to-all-start.2 = ((bf16[32,64,128]{2,1,0:T(8,128)(2,1)}), bf16[32,64,128]{2,1,0:T(8,128)(2,1)S(1)}, u32[]{:S(2)}, u32[]{:S(2)}) async-start(bf16[32,64,128]{2,1,0:T(8,128)(2,1)} %bitcast.7), calls=%async_computation.2 | async-start | bytes 1048576 | tf_op jit(solution)/shard_map/all_to_all | solution.py:107
  130.8 4.6 %fusion.1 = bf16[2048,256]{0,1:T(8,128)(2,1)} fusion(bf16[8,128,256]{2,1,0:T(8,128)(2,1)} %copy-done.7, bf16[8,128,2048]{2,1,0:T(8,128)(2,1)} %all-gather.2.cloned.1.call-done), kind=kOutput, calls=%fused_computation.2 | convolution fusion | flops 1074266112 | bytes 5767168 | tf_op jit(solution)/shard_map/dot_general | solution.py:17
  135.5 2.3 %copy.13 = bf16[2048,256]{1,0:T(8,128)(2,1)} copy(bf16[2048,256]{0,1:T(8,128)(2,1)} %fusion.1) | data formatting | bytes 2097152 | tf_op jit(solution)/shard_map/convert_element_type | solution.py:133
  137.8 7.1 %all-to-all-done.2.part_ref = bf16[32,64,128]{2,1,0:T(8,128)(2,1)S(1)} async-done(((bf16[32,64,128]{2,1,0:T(8,128)(2,1)}), bf16[32,64,128]{2,1,0:T(8,128)(2,1)S(1)}, u32[]{:S(2)}, u32[]{:S(2)}) %all-to-all-start.2) | async-done | bytes 524320 | tf_op jit(solution)/shard_map/all_to_all | solution.py:107
  144.9 7.9 %all-to-all-start.7 = ((bf16[32,64,256]{2,1,0:T(8,128)(2,1)}), bf16[32,64,256]{2,1,0:T(8,128)(2,1)}, u32[]{:S(2)}, u32[]{:S(2)}) async-start(bf16[32,64,256]{2,1,0:T(8,128)(2,1)} %bitcast.40), calls=%async_computation.7 | async-start | bytes 2097152 | tf_op jit(solution)/shard_map/all_to_all | solution.py:107
  153.7 23.8 %all-to-all-done.7.part_ref = bf16[32,64,256]{2,1,0:T(8,128)(2,1)} async-done(((bf16[32,64,256]{2,1,0:T(8,128)(2,1)}), bf16[32,64,256]{2,1,0:T(8,128)(2,1)}, u32[]{:S(2)}, u32[]{:S(2)}) %all-to-all-start.7) | async-done | bytes 1048608 | tf_op jit(solution)/shard_map/all_to_all | solution.py:107
  177.4 8.5 %all-to-all-start.3 = ((bf16[32,64,128]{2,1,0:T(8,128)(2,1)}), bf16[32,64,128]{2,1,0:T(8,128)(2,1)S(1)}, u32[]{:S(2)}, u32[]{:S(2)}) async-start(bf16[32,64,128]{2,1,0:T(8,128)(2,1)} %copy-done.6), calls=%async_computation.3 | async-start | bytes 1048576 | tf_op jit(solution)/shard_map/all_to_all | solution.py:107
  186.0 1.4 shard_map.82
  187.4 15.5 %all_gather.7 = f32[64,2048]{1,0:T(8,128)} all-gather(f32[64,256]{1,0:T(8,128)S(1)} %shard_map.82), channel_id=1, replica_groups=mesh['seq'=32,'dp'=8] {'dp'}, dimensions={1}, use_global_device_ids=true | all-gather | bytes 589824 | tf_op jit(solution)/shard_map/all_gather | solution.py:138
  202.9 4.4 %shard_map.80 = (bf16[128,2048]{1,0:T(8,128)(2,1)}, bf16[128,2048]{1,0:T(8,128)(2,1)}) custom-call(bf16[128,2048]{1,0:T(8,128)(2,1)S(1)} %bitcast.29, bf16[128,2048]{1,0:T(8,128)(2,1)S(1)} %bitcast.32, bf16[128,2048]{1,0:T(8,128)(2,1)S(1)} %bitcast.35, bf16[8,128,256]{2,1,0:T(8,128)(2,1)S(1)} %all-to-all-done.1.right_ref.v_ref, ...), custom_call_target="tpu_custom_call" | custom-call | flops 335544320 | bytes 4194304 | tf_op jit(solution)/shard_map/pallas_call | solution.py:84
  207.3 1.9 copy.16
  (28 shorter events, 8.7 us)
Async XLA Ops:
  7.2 16.0 %copy-start = (bf16[64,2048]{1,0:T(8,128)(2,1)S(1)}, bf16[64,2048]{1,0:T(8,128)(2,1)}, u32[]{:S(2)}) copy-start(bf16[64,2048]{1,0:T(8,128)(2,1)} %param.9) | copy-start | bytes 786436
  7.2 72.2 %all-gather.2.cloned.1.call-start = ((), (), s32[]{:S(2)}) async-start(), calls=%async_computation.8 | async-start | bytes 4718592 | tf_op jit(solution)/shard_map/all_gather | solution.py:116
  7.9 1.0 copy-start.1
  9.0 1.0 copy-start.4
  11.1 26.4 %all-to-all-start.4 = ((bf16[32,64,128]{2,1,0:T(8,128)(2,1)}), bf16[32,64,128]{2,1,0:T(8,128)(2,1)S(1)}, u32[]{:S(2)}, u32[]{:S(2)}) async-start(bf16[32,64,128]{2,1,0:T(8,128)(2,1)} %bitcast.9), calls=%async_computation.4 | async-start | bytes 1048576 | tf_op jit(solution)/shard_map/all_to_all | solution.py:107
  38.6 32.1 %all-to-all-start = ((bf16[32,64,256]{2,1,0:T(8,128)(2,1)}), bf16[32,64,256]{2,1,0:T(8,128)(2,1)S(1)}, u32[]{:S(2)}, u32[]{:S(2)}) async-start(bf16[32,64,256]{2,1,0:T(8,128)(2,1)} %broadcast_in_dim.12), calls=%async_computation | async-start | bytes 2097152 | tf_op jit(solution)/shard_map/all_to_all | solution.py:107
  70.8 8.6 %copy-start.8 = (bf16[32,64,256]{2,1,0:T(8,128)(2,1)}, bf16[32,64,256]{2,1,0:T(8,128)(2,1)S(1)}, u32[]{:S(2)}) copy-start(bf16[32,64,256]{2,1,0:T(8,128)(2,1)S(1)} %all-to-all-done) | copy-start | bytes 3145732
  70.8 22.3 %all-to-all-start.5 = ((bf16[32,64,128]{2,1,0:T(8,128)(2,1)}), bf16[32,64,128]{2,1,0:T(8,128)(2,1)S(1)}, u32[]{:S(2)}, u32[]{:S(2)}) async-start(bf16[32,64,128]{2,1,0:T(8,128)(2,1)} %shard_map.79), calls=%async_computation.5 | async-start | bytes 1048576 | tf_op jit(solution)/shard_map/all_to_all | solution.py:107
  79.4 22.6 %copy-start.2 = (bf16[1,128,2048]{2,1,0:T(8,128)(2,1)S(1)}, bf16[1,128,2048]{2,1,0:T(8,128)(2,1)}, u32[]{:S(2)}) copy-start(bf16[1,128,2048]{2,1,0:T(8,128)(2,1)} %param.6) | copy-start | bytes 1572868
  79.4 22.5 %copy-start.3 = (bf16[1,128,2048]{2,1,0:T(8,128)(2,1)S(1)}, bf16[1,128,2048]{2,1,0:T(8,128)(2,1)}, u32[]{:S(2)}) copy-start(bf16[1,128,2048]{2,1,0:T(8,128)(2,1)} %param.7) | copy-start | bytes 1572868
  79.4 22.5 %copy-start.5 = (bf16[1,128,2048]{2,1,0:T(8,128)(2,1)S(1)}, bf16[1,128,2048]{2,1,0:T(8,128)(2,1)}, u32[]{:S(2)}) copy-start(bf16[1,128,2048]{2,1,0:T(8,128)(2,1)} %param.8) | copy-start | bytes 1572868
  93.1 18.3 %all-to-all-start.1 = ((bf16[8,128,256]{2,1,0:T(8,128)(2,1)}), bf16[8,128,256]{2,1,0:T(8,128)(2,1)S(1)}, u32[]{:S(2)}, u32[]{:S(2)}) async-start(bf16[8,128,256]{2,1,0:T(8,128)(2,1)} %bitcast.6), calls=%async_computation.1 | async-start | bytes 1048576 | tf_op jit(solution)/shard_map/all_to_all | solution.py:107
  111.4 13.8 %all-to-all-start.6 = ((bf16[8,128,256]{2,1,0:T(8,128)(2,1)}), bf16[8,128,256]{2,1,0:T(8,128)(2,1)S(1)}, u32[]{:S(2)}, u32[]{:S(2)}) async-start(bf16[8,128,256]{2,1,0:T(8,128)(2,1)} %shard_map.81), calls=%async_computation.6 | async-start | bytes 1048576 | tf_op jit(solution)/shard_map/all_to_all | solution.py:107
  125.2 0.8 copy-start.7
  126.0 18.9 %all-to-all-start.2 = ((bf16[32,64,128]{2,1,0:T(8,128)(2,1)}), bf16[32,64,128]{2,1,0:T(8,128)(2,1)S(1)}, u32[]{:S(2)}, u32[]{:S(2)}) async-start(bf16[32,64,128]{2,1,0:T(8,128)(2,1)} %bitcast.7), calls=%async_computation.2 | async-start | bytes 1048576 | tf_op jit(solution)/shard_map/all_to_all | solution.py:107
  144.9 32.5 %all-to-all-start.7 = ((bf16[32,64,256]{2,1,0:T(8,128)(2,1)}), bf16[32,64,256]{2,1,0:T(8,128)(2,1)}, u32[]{:S(2)}, u32[]{:S(2)}) async-start(bf16[32,64,256]{2,1,0:T(8,128)(2,1)} %bitcast.40), calls=%async_computation.7 | async-start | bytes 2097152 | tf_op jit(solution)/shard_map/all_to_all | solution.py:107
  152.9 0.8 copy-start.6
  177.4 25.4 %all-to-all-start.3 = ((bf16[32,64,128]{2,1,0:T(8,128)(2,1)}), bf16[32,64,128]{2,1,0:T(8,128)(2,1)S(1)}, u32[]{:S(2)}, u32[]{:S(2)}) async-start(bf16[32,64,128]{2,1,0:T(8,128)(2,1)} %copy-done.6), calls=%async_computation.3 | async-start | bytes 1048576 | tf_op jit(solution)/shard_map/all_to_all | solution.py:107
Sparse Core Ops, SparseCore 0:
  9.9 38.8 all-gather.1

commit v2 on v1

v2 whole, which is shorter than its diff:
```python
import functools
import math

import jax
import jax.numpy as jnp
from jax import lax
from jax.experimental import pallas as pl
from jax.experimental.pallas import tpu as pltpu
from jax.sharding import PartitionSpec as P

HEAD = 128
F32 = jnp.float32
BF16 = jnp.bfloat16


def dot(a, b, a_dim, b_dim):
    return lax.dot_general(a, b, (((a_dim,), (b_dim,)), ((), ())), preferred_element_type=F32)


def cols(h):
    return slice(h * HEAD, (h + 1) * HEAD)


def span(index, size):
    return pl.ds(pl.multiple_of(index * size, size), size)


def causal_mask(rows):
    t = lax.broadcasted_iota(jnp.int32, (rows, rows), 0)
    s = lax.broadcasted_iota(jnp.int32, (rows, rows), 1)
    return t >= s


def first_kernel(ids, q_ref, g_ref, w_ref, out_ref):
    count, rows, _ = out_ref.shape
    for h in range(q_ref.shape[1] // HEAD):
        state = dot(q_ref[:, cols(h)], g_ref[:, cols(h)], 0, 0).astype(BF16)
        for i in range(HEAD // rows):
            out_ref[h * (HEAD // rows) + i, :, :HEAD] = state[i * rows:(i + 1) * rows, :]
    block = out_ref.shape[2] - HEAD
    own = w_ref[:, span(ids[0], block)]
    for i in range(count):
        out_ref[i, :, HEAD:] = own


def slot_state_kernel(slots, ids, left_ref, *refs):
    rights, (out_ref, whole_ref) = refs[:slots], refs[-2:]
    block = rights[0].shape[1]
    for o, right_ref in enumerate(rights):
        b = ids[0] ^ o
        left = left_ref[:, span(b, block)]
        whole_ref[:, span(b, block)] = right_ref[...]
        for j in range(block // HEAD):
            state = dot(left[:, cols(j)], right_ref[:, cols(j)], 0, 0).astype(BF16)
            out_ref[span(b * (block // HEAD) + j, HEAD), :] = state


def prefix_kernel(reverse, ids, part_ref, *refs):
    out_ref = refs[-1]
    count = part_ref.shape[0]
    total = jnp.zeros(out_ref.shape[1:], F32)
    for step in range(count):
        i = count - 1 - step if reverse else step
        out_ref[i] = total.astype(BF16)
        total = total + part_ref[i, :, :HEAD].astype(F32)


def values_kernel(slots, ids, x_ref, first_ref, *refs):
    outs, (w_ref, res_ref) = refs[-slots - 2:-2], refs[-2:]
    step = pl.program_id(0)
    count, rows = x_ref.shape[:2]

    @pl.when(step == 0)
    def _():
        size = first_ref.shape[1]
        for i in range(first_ref.shape[0]):
            w_ref[i * size:(i + 1) * size, :] = first_ref[i, :, HEAD:]

    x = x_ref[...].reshape(count * rows, x_ref.shape[2])
    res_ref[...] = dot(x, w_ref[...], 1, 0).astype(BF16).reshape(res_ref.shape)
    for o, out_ref in enumerate(outs):
        @pl.when(step == o // count)
        def _(o=o, out_ref=out_ref):
            out_ref[...] = res_ref[(ids[0] ^ o) % count]


def grad_values_kernel(scale, slots, ids, q_ref, k_ref, g_ref, qg_ref, *refs):
    outs = refs[-slots:]
    mask = causal_mask(q_ref.shape[0])
    block = outs[0].shape[1]
    for o, out_ref in enumerate(outs):
        b = ids[0] ^ o
        at = span(b, block)
        qs, ks, gs = q_ref[:, at], k_ref[:, at], g_ref[:, at]
        for j in range(block // HEAD):
            q, k, g = qs[:, cols(j)], ks[:, cols(j)], gs[:, cols(j)]
            state = qg_ref[span(b * (block // HEAD) + j, HEAD), :]
            score = jnp.where(mask, dot(q, k, 1, 1) * scale, 0.0).astype(BF16)
            grad = scale * dot(k, state, 1, 0) + dot(score, g, 0, 0)
            out_ref[:, cols(j)] = grad.astype(BF16)


def grad_key_kernel(scale, ids, q_ref, g_ref, v_ref, qg_ref, *refs):
    gk_ref, score_ref = refs[-2:]
    mask = causal_mask(q_ref.shape[0])
    for h in range(q_ref.shape[1] // HEAD):
        q, g, v = q_ref[:, cols(h)], g_ref[:, cols(h)], v_ref[:, cols(h)]
        score = jnp.where(mask, dot(g, v, 1, 1) * scale, 0.0).astype(BF16)
        score_ref[cols(h), :] = score
        grad = scale * dot(v, qg_ref[cols(h), :], 1, 1) + dot(score, q, 0, 0)
        gk_ref[:, cols(h)] = grad.astype(BF16)


def grad_query_kernel(scale, ids, k_ref, g_ref, score_ref, kv_ref, gq_ref):
    for h in range(k_ref.shape[1] // HEAD):
        grad = scale * dot(g_ref[:, cols(h)], kv_ref[cols(h), :], 1, 1)
        grad = grad + dot(score_ref[cols(h), :], k_ref[:, cols(h)], 1, 0)
        gq_ref[:, cols(h)] = grad.astype(BF16)


def product_kernel(slots, ids, x_ref, *refs):
    pieces, out_ref, held_ref = refs[:slots], refs[-2], refs[-1]

    @pl.when(pl.program_id(0) == 0)
    def _():
        for o, piece in enumerate(pieces):
            held_ref[:, span(ids[0] ^ o, piece.shape[0])] = piece[...].T

    out_ref[0] = dot(held_ref[...], x_ref[...], 1, 0).astype(BF16).T


def parts_sum_kernel(factor, ids, part_ref, *refs):
    total = part_ref[0].astype(F32)
    for i in range(1, part_ref.shape[0]):
        total = total + part_ref[i].astype(F32)
    refs[-1][...] = (total * factor).astype(BF16)


def assemble_kernel(ids, part_ref, out_ref):
    block = part_ref.shape[2]
    for b in range(part_ref.shape[0]):
        out_ref[:, b * block:(b + 1) * block] = part_ref[b].astype(F32)


def call(kernel, shapes, flops, ids, *operands, grid=None, first=None, out_first=None, scratch=(), after=(), through=()):
    out = [jax.ShapeDtypeStruct(s, d) for s, d in shapes]
    moved = sum(x.size * x.dtype.itemsize for x in list(operands) + out)
    whole = lambda s: pl.BlockSpec(s, lambda *_: (0,) * len(s))
    anywhere = pl.BlockSpec(memory_space=pl.ANY)
    in_specs = [whole(x.shape) for x in operands]
    if first is not None:
        in_specs[0] = first
    out_specs = [out_first] if out_first else [whole(s) for s, _ in shapes]
    result = pl.pallas_call(
        kernel,
        out_shape=[jax.ShapeDtypeStruct(x.shape, x.dtype) for x in through] + out,
        grid_spec=pltpu.PrefetchScalarGridSpec(
            num_scalar_prefetch=1,
            grid=grid or (1,),
            in_specs=in_specs + [anywhere] * (len(after) + len(through)),
            out_specs=[anywhere] * len(through) + out_specs,
            scratch_shapes=list(scratch),
        ),
        input_output_aliases={1 + len(operands) + len(after) + i: i for i in range(len(through))},
        compiler_params=pltpu.CompilerParams(vmem_limit_bytes=16 * 2**20),
        cost_estimate=pl.CostEstimate(flops=flops, bytes_accessed=moved, transcendentals=0),
    )(ids, *operands, *after, *through)
    return result[0] if len(result) == 1 else result


def on_device(inputs, query_rows, key_rows, cotangent, w_value):
    rows, width = inputs.shape[1:]
    width_all = query_rows.shape[2]
    heads = width_all // HEAD
    seq, dp = lax.axis_size("seq"), lax.axis_size("dp")
    pieces = 4
    scale = 1.0 / math.sqrt(HEAD * rows * seq)
    grad_scale = 1.0 / math.sqrt(inputs.shape[0] * dp * rows * seq)
    block = width_all // dp
    q, k, g = query_rows[0], key_rows[0], cotangent[0]
    head_flops = 2 * rows * HEAD * HEAD * heads
    ids = lax.axis_index("dp").astype(jnp.int32)[None]


    def exchange(array):
        return lax.all_to_all(array, "seq", 0, 0, tiled=True)

    def swap_slots(arrays):
        return [
            a if o == 0 else lax.ppermute(a, "dp", [(i, i ^ o) for i in range(dp)])
            for o, a in enumerate(arrays)
        ]

    def sums_of(parts, reverse, through=()):
        return call(
            functools.partial(prefix_kernel, reverse), [((seq, width_all // seq, HEAD), BF16)],
            seq * width_all // seq * HEAD, ids, parts, through=through,
        )

    all_inputs = lax.all_gather(inputs, "dp", axis=0, tiled=True)

    first = exchange(call(
        first_kernel, [((seq, width // seq, HEAD + block), BF16)], head_flops, ids, q, g, w_value
    ))
    qg_sums = sums_of(first, True)
    qg_round = exchange(qg_sums).reshape(width_all, HEAD)

    values = call(
        functools.partial(values_kernel, dp), [((rows, block), BF16)] * dp,
        2 * rows * width * width_all, ids, all_inputs, first, after=(qg_sums,),
        grid=(dp // 2,),
        first=pl.BlockSpec((2, rows, width), lambda i, ids: ((ids[0] // 2) ^ i, 0, 0)),
        scratch=[pltpu.VMEM((width, block), BF16), pltpu.VMEM((2, rows, block), BF16)],
    )
    kv_local, values = call(
        functools.partial(slot_state_kernel, dp),
        [((heads * HEAD, HEAD), BF16), ((rows, width_all), BF16)], head_flops, ids, k,
        *swap_slots(values), after=(qg_round,),
    )
    kv_parts = exchange(kv_local.reshape(seq, -1, HEAD))

    grad_values = call(
        functools.partial(grad_values_kernel, scale, dp), [((rows, block), BF16)] * dp,
        3 * head_flops, ids, q, k, g, qg_round, after=(kv_local,),
    )
    terms = call(
        functools.partial(product_kernel, dp), [((pieces, width // pieces, block), BF16)],
        2 * rows * width * width_all, ids, all_inputs.reshape(dp * rows, width),
        *swap_slots(grad_values),
        grid=(pieces,),
        first=pl.BlockSpec((dp * rows, width // pieces), lambda i, ids: (0, i)),
        out_first=pl.BlockSpec((1, width // pieces, block), lambda i, ids: (i, 0, 0)),
        scratch=[pltpu.VMEM((block, dp * rows), BF16)],
    )
    terms, kv_sums = sums_of(kv_parts, False, (terms,))
    grad_key, score = call(
        functools.partial(grad_key_kernel, scale),
        [((rows, width_all), BF16), ((heads * HEAD, rows), BF16)],
        3 * head_flops, ids, q, g, values, qg_round, after=(kv_sums,),
    )
    parts = exchange(terms.reshape(seq, width // seq, block))
    kv_sums, summed = call(
        functools.partial(parts_sum_kernel, grad_scale), [((width // seq, block), BF16)],
        0, ids, parts, after=(score,), through=(kv_sums,),
    )
    kv_round = exchange(kv_sums).reshape(width_all, HEAD)
    grad_weight = call(
        assemble_kernel, [((width // seq, width_all), F32)], 0, ids, lax.all_gather(summed, "dp")
    )

    grad_query = call(
        functools.partial(grad_query_kernel, scale), [((rows, width_all), BF16)],
        2 * head_flops, ids, k, g, score, kv_round,
    )
    return grad_query[None], grad_key[None], grad_weight


def solution(mesh):
    placed = (
        P("dp", "seq", None),
        P("dp", "seq", None),
        P("dp", "seq", None),
        P("dp", "seq", None),
        P("seq", None),
    )
    return jax.shard_map(
        on_device,
        mesh=mesh,
        in_specs=placed,
        out_specs=(P("dp", "seq", None), P("dp", "seq", None), P("seq", None)),
        check_vma=False,
    )
```

time: 217 us -> 188 us (0.87)
  waiting for transfers between devices: 94.5 us -> 32.5 us
  blocking collectives: 15.5 us -> 62.6 us
  starting transfers between devices: 62.5 us -> 52.3 us
  matrix products: 8.56 us -> 0 us
  Pallas kernels: 10.7 us -> 16.3 us
  local copies, waits for them, and re-layouts: 9.99 us -> 7.41 us
    all_to_all x8 -> x4, waiting for transfers between devices: 93.8 us -> 22.7 us  [exchange(): return lax.all_to_all(array, 'seq', 0, 0, tiled=True)]
    all_to_all x0 -> x1, blocking collectives: none -> 48.5 us  [exchange(): return lax.all_to_all(array, 'seq', 0, 0, tiled=True)]
    all_to_all x8 -> x4, starting transfers between devices: 62.5 us -> 35 us  [exchange(): return lax.all_to_all(array, 'seq', 0, 0, tiled=True)]
    ppermute x0 -> x14, starting transfers between devices: none -> 17.2 us  [swap_slots(): lax.ppermute(a, 'dp', [(i, i ^ o) for i in range(dp)])]
    ppermute x0 -> x14, waiting for transfers between devices: none -> 9.14 us  [swap_slots(): lax.ppermute(a, 'dp', [(i, i ^ o) for i in range(dp)])]
    dot_general x2 -> x0, matrix products: 8.56 us -> none  [the longest x1 4.64 us: dot(): lax.dot_general(a, b, (((a_dim,), (b_dim,)), ((), ())), preferred_element...]
    pallas_call x7 -> x11, Pallas kernels: 10.7 us -> 16.3 us  [call(): pl.pallas_call(kernel, out_shape=[jax.ShapeDtypeStruct(x.shape, x.dtype)...]
    convert_element_type x2 -> x0, local copies, waits for them, and re-layouts: 3.28 us -> none  [the longest x1 2.28 us: on_device(): product = dot(all_inputs, grad_values, 0, 0).astype(BF16)]
  transfers between devices with their start and end apart: 9 -> 19, of which waited for: 7 -> 11; matrix products, arithmetic and copies ran while one was open for 6% -> 0% of each run, Pallas kernels for 3% -> 6%
where the time goes in v2:
time: 188 us; the launch traced here: 185 us
  blocking collectives  62.6 us (33%)
  starting transfers between devices  52.3 us (28%)
  waiting for transfers between devices  32.5 us (17%)
  Pallas kernels  16.3 us (9%)
  between operations  14.2 us (8%)
  local copies, waits for them, and re-layouts  7.41 us (4%)
    all_to_all x1, blocking collectives, exchange(): return lax.all_to_all(array, 'seq', 0, 0, tiled=True)  48.5 us
    all_to_all x4, starting transfers between devices, exchange(): return lax.all_to_all(array, 'seq', 0, 0, tiled=True)  35 us
    all_to_all x4, waiting for transfers between devices, exchange(): return lax.all_to_all(array, 'seq', 0, 0, tiled=True)  22.7 us
    ppermute x14, starting transfers between devices, swap_slots(): lax.ppermute(a, 'dp', [(i, i ^ o) for i in range(dp)])  17.2 us
    pallas_call x11, Pallas kernels, call(): pl.pallas_call(kernel, out_shape=[jax.ShapeDtypeStruct(x.shape, x.dtype)...  16.3 us
    all_gather x1, blocking collectives, on_device(): lax.all_gather(summed, 'dp')  14.1 us
    ppermute x14, waiting for transfers between devices, swap_slots(): lax.ppermute(a, 'dp', [(i, i ^ o) for i in range(dp)])  9.14 us
    unnamed x16, local copies, waits for them, and re-layouts  7.41 us
  transfers between devices with their start and end apart: 19, of which 11 were waited for; matrix products, arithmetic and copies ran while one was open for 0% of the time, Pallas kernels for 6%

profile of v2, /device:TPU:1, one launch (start us, length us, event | category | flops | bytes accessed | tf_op | source)
XLA Modules:
  0.0 185.3 jit_solution(110408685169751560)
XLA Ops:
  11.3 48.5 %all_to_all.25.part_ref.first_ref = bf16[32,64,384]{2,1,0:T(8,128)(2,1)S(1)} all-to-all(bf16[32,64,384]{2,1,0:T(8,128)(2,1)S(1)} %shard_map.76), channel_id=1, replica_groups=mesh['seq'=32,'dp'=8] {'seq'}, dimensions={0} | all-to-all | bytes 3145728 | tf_op jit(solution)/shard_map/all_to_all | solution.py:186
  60.7 8.1 %all-to-all-start.1 = ((bf16[32,64,128]{2,1,0:T(8,128)(2,1)}), bf16[32,64,128]{2,1,0:T(8,128)(2,1)S(1)}, u32[]{:S(2)}, u32[]{:S(2)}) async-start(bf16[32,64,128]{2,1,0:T(8,128)(2,1)} %shard_map.77.refs_0_), calls=%async_computation.1 | async-start | bytes 1048576 | tf_op jit(solution)/shard_map/all_to_all | solution.py:186
  68.8 2.2 %copy-done = bf16[8,128,2048]{2,1,0:T(8,128)(2,1)S(1)} copy-done((bf16[8,128,2048]{2,1,0:T(8,128)(2,1)S(1)}, bf16[8,128,2048]{2,1,0:T(8,128)(2,1)}, u32[]{:S(2)}) %copy-start) | copy-done | bytes 4194328
  71.0 2.0 %shard_map.78 = (bf16[128,256]{1,0:T(8,128)(2,1)S(1)}, bf16[128,256]{1,0:T(8,128)(2,1)S(1)}, bf16[128,256]{1,0:T(8,128)(2,1)S(1)}, bf16[128,256]{1,0:T(8,128)(2,...) custom-call(s32[1]{0:T(128)} %bitcast.ids, ...), custom_call_target="tpu_custom_call" | custom-call | flops 1073741824 | bytes 6291456 | tf_op jit(solution)/shard_map/pallas_call | solution.py:154
  73.1 1.3 collective-permute-start
  76.0 2.7 %collective-permute-start.3 = (bf16[128,256]{1,0:T(8,128)(2,1)S(1)}, bf16[128,256]{1,0:T(8,128)(2,1)S(1)}, u32[]{:S(2)}, u32[]{:S(2)}) collective-permute-start(bf16[128,256]{1,0:T(8,128)(2,1)S(1)} %get-tuple-element.31), channel_id=1, source_target_pairs={{0,4},{1,5},{2,6},{3,7},{4,0},{5,1},{6,2},{7,3},{8,12},{9,13},{10,... | collective-permute-start | bytes 196616 | tf_op jit(solution)/shard_map/ppermute | solution.py:190
  79.3 2.5 %collective-permute-start.5 = (bf16[128,256]{1,0:T(8,128)(2,1)S(1)}, bf16[128,256]{1,0:T(8,128)(2,1)S(1)}, u32[]{:S(2)}, u32[]{:S(2)}) collective-permute-start(bf16[128,256]{1,0:T(8,128)(2,1)S(1)} %get-tuple-element.33), channel_id=1, source_target_pairs={{0,6},{1,7},{2,4},{3,5},{4,2},{5,3},{6,0},{7,1},{8,14},{9,15},{10,... | collective-permute-start | bytes 196616 | tf_op jit(solution)/shard_map/ppermute | solution.py:190
  83.0 1.9 %collective-permute-done.4.refs_5_ = bf16[128,256]{1,0:T(8,128)(2,1)S(1)} collective-permute-done((bf16[128,256]{1,0:T(8,128)(2,1)S(1)}, bf16[128,256]{1,0:T(8,128)(2,1)S(1)}, u32[]{:S(2)}, u32[]{:S(2)}) %collective-permute-start.4) | collective-permute-done | bytes 65568 | tf_op jit(solution)/shard_map/ppermute | solution.py:190
  84.9 1.3 collective-permute-done.5.refs_6_
  86.2 1.3 collective-permute-done.6.refs_7_
  88.7 9.5 %all-to-all-start.2 = ((bf16[32,64,128]{2,1,0:T(8,128)(2,1)}), bf16[32,64,128]{2,1,0:T(8,128)(2,1)S(1)}, u32[]{:S(2)}, u32[]{:S(2)}) async-start(bf16[32,64,128]{2,1,0:T(8,128)(2,1)} %bitcast.5), calls=%async_computation.2 | async-start | bytes 1048576 | tf_op jit(solution)/shard_map/all_to_all | solution.py:186
  100.3 2.8 %collective-permute-start.11 = (bf16[128,256]{1,0:T(8,128)(2,1)S(1)}, bf16[128,256]{1,0:T(8,128)(2,1)S(1)}, u32[]{:S(2)}, u32[]{:S(2)}) collective-permute-start(bf16[128,256]{1,0:T(8,128)(2,1)S(1)} %get-tuple-element.42), channel_id=1, source_target_pairs={{0,5},{1,4},{2,7},{3,6},{4,1},{5,0},{6,3},{7,2},{8,13},{9,12},{10,... | collective-permute-start | bytes 196616 | tf_op jit(solution)/shard_map/ppermute | solution.py:190
  103.6 1.8 collective-permute-start.13
  108.4 1.4 collective-permute-done.13.refs_7_
  109.9 1.8 collective-permute-done.9.refs_3_
  111.7 2.2 %copy-done.1 = bf16[8,128,2048]{2,1,0:T(8,128)(2,1)S(1)} copy-done((bf16[8,128,2048]{2,1,0:T(8,128)(2,1)S(1)}, bf16[8,128,2048]{2,1,0:T(8,128)(2,1)}, u32[]{:S(2)}) %copy-start.1) | copy-done | bytes 4194328
  113.9 3.4 %shard_map.81.refs_0_ = bf16[4,512,256]{2,1,0:T(8,128)(2,1)} custom-call(s32[1]{0:T(128)} %bitcast.ids, bf16[1024,2048]{1,0:T(8,128)(2,1)S(1)} %bitcast.12, bf16[128,256]{1,0:T(8,128)(2,1)S(1)} %get-tuple-element.37.refs_0_, bf16[128,256]{1,0:T(8,128)(2,1)S(1)} %collective-permute-done.7.refs_1_, bf16[128,256]{1,0:T(8,128)(2,1)S(1)} %collective-permute-done.8.refs_2_, ...), custom_call_target="tpu_custom_call" | custom-call | flops 1073741824 | bytes 5767168 | tf_op jit(solution)/shard_map/pallas_call | solution.py:154
  118.2 9.3 %all-to-all-start.3 = ((bf16[32,64,256]{2,1,0:T(8,128)(2,1)}), bf16[32,64,256]{2,1,0:T(8,128)(2,1)}, u32[]{:S(2)}, u32[]{:S(2)}) async-start(bf16[32,64,256]{2,1,0:T(8,128)(2,1)} %bitcast.7), calls=%async_computation.3 | async-start | bytes 2097152 | tf_op jit(solution)/shard_map/all_to_all | solution.py:186
  127.5 3.0 %shard_map.83 = (bf16[128,2048]{1,0:T(8,128)(2,1)}, bf16[2048,128]{1,0:T(8,128)(2,1)S(1)}) custom-call(s32[1]{0:T(128)} %bitcast.ids, bf16[128,2048]{1,0:T(8,128)(2,1)S(1)} %bitcast.25, bf16[128,2048]{1,0:T(8,128)(2,1)S(1)} %bitcast.18, bf16[128,2048]{1,0:T(8,128)(2,1)S(1)} %get-tuple-element.35.v_ref, bf16[2048,128]{1,0:T(8,128)(2,1)S(1)} %bitcast.15, ...), custom_call_target="tpu_custom_call" | custom-call | flops 201326592 | bytes 3145728 | tf_op jit(solution)/shard_map/pallas_call | solution.py:154
  130.6 22.1 %all-to-all-done.3.part_ref = bf16[32,64,256]{2,1,0:T(8,128)(2,1)} async-done(((bf16[32,64,256]{2,1,0:T(8,128)(2,1)}), bf16[32,64,256]{2,1,0:T(8,128)(2,1)}, u32[]{:S(2)}, u32[]{:S(2)}) %all-to-all-start.3) | async-done | bytes 1048608 | tf_op jit(solution)/shard_map/all_to_all | solution.py:186
  152.7 1.4 shard_map.84
  154.1 8.1 %all-to-all-start.4 = ((bf16[32,64,128]{2,1,0:T(8,128)(2,1)}), bf16[32,64,128]{2,1,0:T(8,128)(2,1)S(1)}, u32[]{:S(2)}, u32[]{:S(2)}) async-start(bf16[32,64,128]{2,1,0:T(8,128)(2,1)} %get-tuple-element.48), calls=%async_computation.4 | async-start | bytes 1048576 | tf_op jit(solution)/shard_map/all_to_all | solution.py:186
  162.2 14.1 %all-gather = bf16[512,256]{1,0:T(8,128)(2,1)S(1)} all-gather(bf16[64,256]{1,0:T(8,128)(2,1)S(1)} %get-tuple-element.50), channel_id=2, replica_groups=mesh['seq'=32,'dp'=8] {'dp'}, dimensions={0}, use_global_device_ids=true | all-gather | bytes 294912 | tf_op jit(solution)/shard_map/all_gather | solution.py:248
  177.1 1.4 shard_map.85
  (44 shorter events, 16.9 us)
Async XLA Ops:
  7.2 61.6 %all-gather.3.cloned.1.call-start = ((), (), s32[]{:S(2)}) async-start(), calls=%async_computation.5 | async-start | bytes 4718592 | tf_op jit(solution)/shard_map/all_gather | solution.py:200
  60.7 22.1 %all-to-all-start.1 = ((bf16[32,64,128]{2,1,0:T(8,128)(2,1)}), bf16[32,64,128]{2,1,0:T(8,128)(2,1)S(1)}, u32[]{:S(2)}, u32[]{:S(2)}) async-start(bf16[32,64,128]{2,1,0:T(8,128)(2,1)} %shard_map.77.refs_0_), calls=%async_computation.1 | async-start | bytes 1048576 | tf_op jit(solution)/shard_map/all_to_all | solution.py:186
  68.8 2.2 %copy-start = (bf16[8,128,2048]{2,1,0:T(8,128)(2,1)S(1)}, bf16[8,128,2048]{2,1,0:T(8,128)(2,1)}, u32[]{:S(2)}) copy-start(bf16[8,128,2048]{2,1,0:T(8,128)(2,1)} %all-gather.3.cloned.1.call-done.x_ref) | copy-start | bytes 12582916
  71.0 16.5 %copy-start.4 = (bf16[1,128,2048]{2,1,0:T(8,128)(2,1)S(1)}, bf16[1,128,2048]{2,1,0:T(8,128)(2,1)}, u32[]{:S(2)}) copy-start(bf16[1,128,2048]{2,1,0:T(8,128)(2,1)} %param.7) | copy-start | bytes 1572868
  73.0 25.2 %copy-start.3 = (bf16[1,128,2048]{2,1,0:T(8,128)(2,1)S(1)}, bf16[1,128,2048]{2,1,0:T(8,128)(2,1)}, u32[]{:S(2)}) copy-start(bf16[1,128,2048]{2,1,0:T(8,128)(2,1)} %param.8) | copy-start | bytes 1572868
  73.0 25.2 %copy-start.6 = (bf16[1,128,2048]{2,1,0:T(8,128)(2,1)S(1)}, bf16[1,128,2048]{2,1,0:T(8,128)(2,1)}, u32[]{:S(2)}) copy-start(bf16[1,128,2048]{2,1,0:T(8,128)(2,1)} %param.6) | copy-start | bytes 1572868
  73.1 6.3 %collective-permute-start = (bf16[128,256]{1,0:T(8,128)(2,1)S(1)}, bf16[128,256]{1,0:T(8,128)(2,1)S(1)}, u32[]{:S(2)}, u32[]{:S(2)}) collective-permute-start(bf16[128,256]{1,0:T(8,128)(2,1)S(1)} %get-tuple-element.28), channel_id=1, source_target_pairs={{0,1},{1,0},{2,3},{3,2},{4,5},{5,4},{6,7},{7,6},{8,9},{9,8},{10,11... | collective-permute-start | bytes 196616 | tf_op jit(solution)/shard_map/ppermute | solution.py:190
  74.3 7.5 %collective-permute-start.1 = (bf16[128,256]{1,0:T(8,128)(2,1)S(1)}, bf16[128,256]{1,0:T(8,128)(2,1)S(1)}, u32[]{:S(2)}, u32[]{:S(2)}) collective-permute-start(bf16[128,256]{1,0:T(8,128)(2,1)S(1)} %get-tuple-element.29), channel_id=1, source_target_pairs={{0,2},{1,3},{2,0},{3,1},{4,6},{5,7},{6,4},{7,5},{8,10},{9,11},{10,... | collective-permute-start | bytes 196616 | tf_op jit(solution)/shard_map/ppermute | solution.py:190
  75.5 7.3 %collective-permute-start.2 = (bf16[128,256]{1,0:T(8,128)(2,1)S(1)}, bf16[128,256]{1,0:T(8,128)(2,1)S(1)}, u32[]{:S(2)}, u32[]{:S(2)}) collective-permute-start(bf16[128,256]{1,0:T(8,128)(2,1)S(1)} %get-tuple-element.30), channel_id=1, source_target_pairs={{0,3},{1,2},{2,1},{3,0},{4,7},{5,6},{6,5},{7,4},{8,11},{9,10},{10,... | collective-permute-start | bytes 196616 | tf_op jit(solution)/shard_map/ppermute | solution.py:190
  76.0 6.9 %collective-permute-start.3 = (bf16[128,256]{1,0:T(8,128)(2,1)S(1)}, bf16[128,256]{1,0:T(8,128)(2,1)S(1)}, u32[]{:S(2)}, u32[]{:S(2)}) collective-permute-start(bf16[128,256]{1,0:T(8,128)(2,1)S(1)} %get-tuple-element.31), channel_id=1, source_target_pairs={{0,4},{1,5},{2,6},{3,7},{4,0},{5,1},{6,2},{7,3},{8,12},{9,13},{10,... | collective-permute-start | bytes 196616 | tf_op jit(solution)/shard_map/ppermute | solution.py:190
  78.8 6.1 %collective-permute-start.4 = (bf16[128,256]{1,0:T(8,128)(2,1)S(1)}, bf16[128,256]{1,0:T(8,128)(2,1)S(1)}, u32[]{:S(2)}, u32[]{:S(2)}) collective-permute-start(bf16[128,256]{1,0:T(8,128)(2,1)S(1)} %get-tuple-element.32), channel_id=1, source_target_pairs={{0,5},{1,4},{2,7},{3,6},{4,1},{5,0},{6,3},{7,2},{8,13},{9,12},{10,... | collective-permute-start | bytes 196616 | tf_op jit(solution)/shard_map/ppermute | solution.py:190
  79.3 6.9 %collective-permute-start.5 = (bf16[128,256]{1,0:T(8,128)(2,1)S(1)}, bf16[128,256]{1,0:T(8,128)(2,1)S(1)}, u32[]{:S(2)}, u32[]{:S(2)}) collective-permute-start(bf16[128,256]{1,0:T(8,128)(2,1)S(1)} %get-tuple-element.33), channel_id=1, source_target_pairs={{0,6},{1,7},{2,4},{3,5},{4,2},{5,3},{6,0},{7,1},{8,14},{9,15},{10,... | collective-permute-start | bytes 196616 | tf_op jit(solution)/shard_map/ppermute | solution.py:190
  81.8 5.7 %collective-permute-start.6 = (bf16[128,256]{1,0:T(8,128)(2,1)S(1)}, bf16[128,256]{1,0:T(8,128)(2,1)S(1)}, u32[]{:S(2)}, u32[]{:S(2)}) collective-permute-start(bf16[128,256]{1,0:T(8,128)(2,1)S(1)} %get-tuple-element.34), channel_id=1, source_target_pairs={{0,7},{1,6},{2,5},{3,4},{4,3},{5,2},{6,1},{7,0},{8,15},{9,14},{10,... | collective-permute-start | bytes 196616 | tf_op jit(solution)/shard_map/ppermute | solution.py:190
  88.7 28.6 %all-to-all-start.2 = ((bf16[32,64,128]{2,1,0:T(8,128)(2,1)}), bf16[32,64,128]{2,1,0:T(8,128)(2,1)S(1)}, u32[]{:S(2)}, u32[]{:S(2)}) async-start(bf16[32,64,128]{2,1,0:T(8,128)(2,1)} %bitcast.5), calls=%async_computation.2 | async-start | bytes 1048576 | tf_op jit(solution)/shard_map/all_to_all | solution.py:186
  99.2 7.0 %collective-permute-start.10 = (bf16[128,256]{1,0:T(8,128)(2,1)S(1)}, bf16[128,256]{1,0:T(8,128)(2,1)S(1)}, u32[]{:S(2)}, u32[]{:S(2)}) collective-permute-start(bf16[128,256]{1,0:T(8,128)(2,1)S(1)} %get-tuple-element.41), channel_id=1, source_target_pairs={{0,4},{1,5},{2,6},{3,7},{4,0},{5,1},{6,2},{7,3},{8,12},{9,13},{10,... | collective-permute-start | bytes 196616 | tf_op jit(solution)/shard_map/ppermute | solution.py:190
  100.3 6.4 %collective-permute-start.11 = (bf16[128,256]{1,0:T(8,128)(2,1)S(1)}, bf16[128,256]{1,0:T(8,128)(2,1)S(1)}, u32[]{:S(2)}, u32[]{:S(2)}) collective-permute-start(bf16[128,256]{1,0:T(8,128)(2,1)S(1)} %get-tuple-element.42), channel_id=1, source_target_pairs={{0,5},{1,4},{2,7},{3,6},{4,1},{5,0},{6,3},{7,2},{8,13},{9,12},{10,... | collective-permute-start | bytes 196616 | tf_op jit(solution)/shard_map/ppermute | solution.py:190
  103.1 5.3 %collective-permute-start.12 = (bf16[128,256]{1,0:T(8,128)(2,1)S(1)}, bf16[128,256]{1,0:T(8,128)(2,1)S(1)}, u32[]{:S(2)}, u32[]{:S(2)}) collective-permute-start(bf16[128,256]{1,0:T(8,128)(2,1)S(1)} %get-tuple-element.43), channel_id=1, source_target_pairs={{0,6},{1,7},{2,4},{3,5},{4,2},{5,3},{6,0},{7,1},{8,14},{9,15},{10,... | collective-permute-start | bytes 196616 | tf_op jit(solution)/shard_map/ppermute | solution.py:190
  103.6 6.2 %collective-permute-start.13 = (bf16[128,256]{1,0:T(8,128)(2,1)S(1)}, bf16[128,256]{1,0:T(8,128)(2,1)S(1)}, u32[]{:S(2)}, u32[]{:S(2)}) collective-permute-start(bf16[128,256]{1,0:T(8,128)(2,1)S(1)} %get-tuple-element.44), channel_id=1, source_target_pairs={{0,7},{1,6},{2,5},{3,4},{4,3},{5,2},{6,1},{7,0},{8,15},{9,14},{10,... | collective-permute-start | bytes 196616 | tf_op jit(solution)/shard_map/ppermute | solution.py:190
  105.5 4.3 %collective-permute-start.7 = (bf16[128,256]{1,0:T(8,128)(2,1)S(1)}, bf16[128,256]{1,0:T(8,128)(2,1)S(1)}, u32[]{:S(2)}, u32[]{:S(2)}) collective-permute-start(bf16[128,256]{1,0:T(8,128)(2,1)S(1)} %get-tuple-element.38), channel_id=1, source_target_pairs={{0,1},{1,0},{2,3},{3,2},{4,5},{5,4},{6,7},{7,6},{8,9},{9,8},{10,11... | collective-permute-start | bytes 196616 | tf_op jit(solution)/shard_map/ppermute | solution.py:190
  106.2 3.7 %collective-permute-start.8 = (bf16[128,256]{1,0:T(8,128)(2,1)S(1)}, bf16[128,256]{1,0:T(8,128)(2,1)S(1)}, u32[]{:S(2)}, u32[]{:S(2)}) collective-permute-start(bf16[128,256]{1,0:T(8,128)(2,1)S(1)} %get-tuple-element.39), channel_id=1, source_target_pairs={{0,2},{1,3},{2,0},{3,1},{4,6},{5,7},{6,4},{7,5},{8,10},{9,11},{10,... | collective-permute-start | bytes 196616 | tf_op jit(solution)/shard_map/ppermute | solution.py:190
  106.7 5.0 %collective-permute-start.9 = (bf16[128,256]{1,0:T(8,128)(2,1)S(1)}, bf16[128,256]{1,0:T(8,128)(2,1)S(1)}, u32[]{:S(2)}, u32[]{:S(2)}) collective-permute-start(bf16[128,256]{1,0:T(8,128)(2,1)S(1)} %get-tuple-element.40), channel_id=1, source_target_pairs={{0,3},{1,2},{2,1},{3,0},{4,7},{5,6},{6,5},{7,4},{8,11},{9,10},{10,... | collective-permute-start | bytes 196616 | tf_op jit(solution)/shard_map/ppermute | solution.py:190
  111.7 2.2 %copy-start.1 = (bf16[8,128,2048]{2,1,0:T(8,128)(2,1)S(1)}, bf16[8,128,2048]{2,1,0:T(8,128)(2,1)}, u32[]{:S(2)}) copy-start(bf16[8,128,2048]{2,1,0:T(8,128)(2,1)} %all-gather.3.cloned.1.call-done.x_ref) | copy-start | bytes 12582916
  118.2 34.5 %all-to-all-start.3 = ((bf16[32,64,256]{2,1,0:T(8,128)(2,1)}), bf16[32,64,256]{2,1,0:T(8,128)(2,1)}, u32[]{:S(2)}, u32[]{:S(2)}) async-start(bf16[32,64,256]{2,1,0:T(8,128)(2,1)} %bitcast.7), calls=%async_computation.3 | async-start | bytes 2097152 | tf_op jit(solution)/shard_map/all_to_all | solution.py:186
  154.1 23.0 %all-to-all-start.4 = ((bf16[32,64,128]{2,1,0:T(8,128)(2,1)}), bf16[32,64,128]{2,1,0:T(8,128)(2,1)S(1)}, u32[]{:S(2)}, u32[]{:S(2)}) async-start(bf16[32,64,128]{2,1,0:T(8,128)(2,1)} %get-tuple-element.48), calls=%async_computation.4 | async-start | bytes 1048576 | tf_op jit(solution)/shard_map/all_to_all | solution.py:186
  (3 other events, 3.0 us)
Sparse Core Ops, SparseCore 0:
  9.9 38.8 all-gather.2

commit v3 on v2

--- a/solution.py
+++ b/solution.py
@@ -9,6 +9,7 @@
 from jax.sharding import PartitionSpec as P
 
 HEAD = 128
+Z = 8
 F32 = jnp.float32
 BF16 = jnp.bfloat16
 
@@ -173,7 +174,9 @@
     width_all = query_rows.shape[2]
     heads = width_all // HEAD
     seq, dp = lax.axis_size("seq"), lax.axis_size("dp")
-    pieces = 4
+    y_count = seq // Z
+    planes = [[y * Z + z for z in range(Z)] for y in range(y_count)]
+    columns = [[y * Z + z for y in range(y_count)] for z in range(Z)]
     scale = 1.0 / math.sqrt(HEAD * rows * seq)
     grad_scale = 1.0 / math.sqrt(inputs.shape[0] * dp * rows * seq)
     block = width_all // dp
@@ -182,8 +185,8 @@
     ids = lax.axis_index("dp").astype(jnp.int32)[None]
 
 
-    def exchange(array):
-        return lax.all_to_all(array, "seq", 0, 0, tiled=True)
+    def exchange(array, groups=None):
+        return lax.all_to_all(array, "seq", 0, 0, axis_index_groups=groups, tiled=True)
 
     def swap_slots(arrays):
         return [
@@ -224,12 +227,12 @@
         3 * head_flops, ids, q, k, g, qg_round, after=(kv_local,),
     )
     terms = call(
-        functools.partial(product_kernel, dp), [((pieces, width // pieces, block), BF16)],
+        functools.partial(product_kernel, dp), [((y_count, width // y_count, block), BF16)],
         2 * rows * width * width_all, ids, all_inputs.reshape(dp * rows, width),
         *swap_slots(grad_values),
-        grid=(pieces,),
-        first=pl.BlockSpec((dp * rows, width // pieces), lambda i, ids: (0, i)),
-        out_first=pl.BlockSpec((1, width // pieces, block), lambda i, ids: (i, 0, 0)),
+        grid=(y_count,),
+        first=pl.BlockSpec((dp * rows, width // y_count), lambda i, ids: (0, i)),
+        out_first=pl.BlockSpec((1, width // y_count, block), lambda i, ids: (i, 0, 0)),
         scratch=[pltpu.VMEM((block, dp * rows), BF16)],
     )
     terms, kv_sums = sums_of(kv_parts, False, (terms,))
@@ -238,12 +241,15 @@
         [((rows, width_all), BF16), ((heads * HEAD, rows), BF16)],
         3 * head_flops, ids, q, g, values, qg_round, after=(kv_sums,),
     )
-    parts = exchange(terms.reshape(seq, width // seq, block))
-    kv_sums, summed = call(
+    kv_round = exchange(kv_sums).reshape(width_all, HEAD)
+    term = lax.psum_scatter(
+        terms.reshape(width, block), "seq", scatter_dimension=0, axis_index_groups=columns, tiled=True
+    )
+    parts = exchange(term.reshape(Z, width // seq, block), planes)
+    summed = call(
         functools.partial(parts_sum_kernel, grad_scale), [((width // seq, block), BF16)],
-        0, ids, parts, after=(score,), through=(kv_sums,),
-    )
-    kv_round = exchange(kv_sums).reshape(width_all, HEAD)
+        0, ids, parts, after=(kv_round, score),
+    )
     grad_weight = call(
         assemble_kernel, [((width // seq, width_all), F32)], 0, ids, lax.all_gather(summed, "dp")
     )

time: 188 us -> 186 us (0.989); the launches traced: 185 us -> 186 us
  blocking collectives: 62.6 us -> 87.8 us
  waiting for transfers between devices: 32.5 us -> 18.3 us
  starting transfers between devices: 52.3 us -> 40.8 us
  local copies, waits for them, and re-layouts: 7.41 us -> 10.3 us
  Pallas kernels: 16.3 us -> 14.2 us
    all_to_all x1 -> x2, blocking collectives: 48.5 us -> 71.5 us  [exchange(): lax.all_to_all(array, 'seq', 0, 0, axis_index_groups=groups, tiled=True)]
    all_to_all x4 -> x3, waiting for transfers between devices: 22.7 us -> 3.28 us  [exchange(): lax.all_to_all(array, 'seq', 0, 0, axis_index_groups=groups, tiled=True)]
    all_to_all x4 -> x3, starting transfers between devices: 35 us -> 23.5 us  [exchange(): lax.all_to_all(array, 'seq', 0, 0, axis_index_groups=groups, tiled=True)]
    reduce_scatter x0 -> x1, waiting for transfers between devices: none -> 5.15 us  [on_device(): lax.psum_scatter(terms.reshape(width, block), 'seq', scatter_dimension=0,...]
    unnamed x16 -> x24, local copies, waits for them, and re-layouts: 7.41 us -> 10.3 us
    all_gather x1, blocking collectives: 14.1 us -> 16.3 us  [on_device(): lax.all_gather(summed, 'dp')]
    pallas_call x11, Pallas kernels: 16.3 us -> 14.2 us  [call(): pl.pallas_call(kernel, out_shape=[jax.ShapeDtypeStruct(x.shape, x.dtype)...]
  transfers between devices with their start and end apart: 19 -> 19, of which waited for: 11 -> 12; matrix products, arithmetic and copies ran while one was open for 0% -> 0% of each run, Pallas kernels for 6% -> 7%
where the time goes in v3:
time: 186 us
  blocking collectives  87.8 us (47%)
  starting transfers between devices  40.8 us (22%)
  waiting for transfers between devices  18.3 us (10%)
  Pallas kernels  14.2 us (8%)
  between operations  14.2 us (8%)
  local copies, waits for them, and re-layouts  10.3 us (6%)
    all_to_all x2, blocking collectives, exchange(): lax.all_to_all(array, 'seq', 0, 0, axis_index_groups=groups, tiled=True)  71.5 us
    all_to_all x3, starting transfers between devices, exchange(): lax.all_to_all(array, 'seq', 0, 0, axis_index_groups=groups, tiled=True)  23.5 us
    ppermute x14, starting transfers between devices, swap_slots(): lax.ppermute(a, 'dp', [(i, i ^ o) for i in range(dp)])  17.2 us
    all_gather x1, blocking collectives, on_device(): lax.all_gather(summed, 'dp')  16.3 us
    pallas_call x11, Pallas kernels, call(): pl.pallas_call(kernel, out_shape=[jax.ShapeDtypeStruct(x.shape, x.dtype)...  14.2 us
    unnamed x24, local copies, waits for them, and re-layouts  10.3 us
    ppermute x14, waiting for transfers between devices, swap_slots(): lax.ppermute(a, 'dp', [(i, i ^ o) for i in range(dp)])  9.14 us
    reduce_scatter x1, waiting for transfers between devices, on_device(): lax.psum_scatter(terms.reshape(width, block), 'seq', scatter_dimension=0,...  5.15 us
  transfers between devices with their start and end apart: 19, of which 12 were waited for; matrix products, arithmetic and copies ran while one was open for 0% of the time, Pallas kernels for 7%

profile of v3, /device:TPU:1, one launch (start us, length us, event | category | flops | bytes accessed | tf_op | source)
XLA Modules:
  0.0 185.6 jit_solution(11240822037246557924)
XLA Ops:
  11.3 48.5 %all_to_all.25.part_ref.first_ref = bf16[32,64,384]{2,1,0:T(8,128)(2,1)S(1)} all-to-all(bf16[32,64,384]{2,1,0:T(8,128)(2,1)S(1)} %shard_map.76), channel_id=1, replica_groups=mesh['seq'=32,'dp'=8] {'seq'}, dimensions={0} | all-to-all | bytes 3145728 | tf_op jit(solution)/shard_map/all_to_all | solution.py:189
  60.7 8.1 %all-to-all-start.1 = ((bf16[32,64,128]{2,1,0:T(8,128)(2,1)}), bf16[32,64,128]{2,1,0:T(8,128)(2,1)S(1)}, u32[]{:S(2)}, u32[]{:S(2)}) async-start(bf16[32,64,128]{2,1,0:T(8,128)(2,1)} %shard_map.77.refs_0_), calls=%async_computation.1 | async-start | bytes 1048576 | tf_op jit(solution)/shard_map/all_to_all | solution.py:189
  68.8 2.2 %copy-done = bf16[8,128,2048]{2,1,0:T(8,128)(2,1)S(1)} copy-done((bf16[8,128,2048]{2,1,0:T(8,128)(2,1)S(1)}, bf16[8,128,2048]{2,1,0:T(8,128)(2,1)}, u32[]{:S(2)}) %copy-start) | copy-done | bytes 4194328
  71.0 2.0 %shard_map.78 = (bf16[128,256]{1,0:T(8,128)(2,1)S(1)}, bf16[128,256]{1,0:T(8,128)(2,1)S(1)}, bf16[128,256]{1,0:T(8,128)(2,1)S(1)}, bf16[128,256]{1,0:T(8,128)(2,...) custom-call(s32[1]{0:T(128)} %bitcast.ids, ...), custom_call_target="tpu_custom_call" | custom-call | flops 1073741824 | bytes 6291456 | tf_op jit(solution)/shard_map/pallas_call | solution.py:155
  73.1 1.3 collective-permute-start
  76.0 2.7 %collective-permute-start.3 = (bf16[128,256]{1,0:T(8,128)(2,1)S(1)}, bf16[128,256]{1,0:T(8,128)(2,1)S(1)}, u32[]{:S(2)}, u32[]{:S(2)}) collective-permute-start(bf16[128,256]{1,0:T(8,128)(2,1)S(1)} %get-tuple-element.29), channel_id=1, source_target_pairs={{0,4},{1,5},{2,6},{3,7},{4,0},{5,1},{6,2},{7,3},{8,12},{9,13},{10,... | collective-permute-start | bytes 196616 | tf_op jit(solution)/shard_map/ppermute | solution.py:193
  79.3 2.5 %collective-permute-start.5 = (bf16[128,256]{1,0:T(8,128)(2,1)S(1)}, bf16[128,256]{1,0:T(8,128)(2,1)S(1)}, u32[]{:S(2)}, u32[]{:S(2)}) collective-permute-start(bf16[128,256]{1,0:T(8,128)(2,1)S(1)} %get-tuple-element.31), channel_id=1, source_target_pairs={{0,6},{1,7},{2,4},{3,5},{4,2},{5,3},{6,0},{7,1},{8,14},{9,15},{10,... | collective-permute-start | bytes 196616 | tf_op jit(solution)/shard_map/ppermute | solution.py:193
  83.0 1.9 %collective-permute-done.4.refs_5_ = bf16[128,256]{1,0:T(8,128)(2,1)S(1)} collective-permute-done((bf16[128,256]{1,0:T(8,128)(2,1)S(1)}, bf16[128,256]{1,0:T(8,128)(2,1)S(1)}, u32[]{:S(2)}, u32[]{:S(2)}) %collective-permute-start.4) | collective-permute-done | bytes 65568 | tf_op jit(solution)/shard_map/ppermute | solution.py:193
  84.9 1.3 collective-permute-done.5.refs_6_
  86.2 1.3 collective-permute-done.6.refs_7_
  89.5 9.5 %all-to-all-start.2 = ((bf16[32,64,128]{2,1,0:T(8,128)(2,1)}), bf16[32,64,128]{2,1,0:T(8,128)(2,1)S(1)}, u32[]{:S(2)}, u32[]{:S(2)}) async-start(bf16[32,64,128]{2,1,0:T(8,128)(2,1)} %bitcast.5), calls=%async_computation.2 | async-start | bytes 1048576 | tf_op jit(solution)/shard_map/all_to_all | solution.py:189
  101.2 2.8 %collective-permute-start.11 = (bf16[128,256]{1,0:T(8,128)(2,1)S(1)}, bf16[128,256]{1,0:T(8,128)(2,1)S(1)}, u32[]{:S(2)}, u32[]{:S(2)}) collective-permute-start(bf16[128,256]{1,0:T(8,128)(2,1)S(1)} %get-tuple-element.40), channel_id=1, source_target_pairs={{0,5},{1,4},{2,7},{3,6},{4,1},{5,0},{6,3},{7,2},{8,13},{9,12},{10,... | collective-permute-start | bytes 196616 | tf_op jit(solution)/shard_map/ppermute | solution.py:193
  104.5 1.8 collective-permute-start.13
  109.2 1.4 collective-permute-done.13.refs_7_
  110.7 1.8 collective-permute-done.9.refs_3_
  112.5 2.2 %copy-done.1 = bf16[8,128,2048]{2,1,0:T(8,128)(2,1)S(1)} copy-done((bf16[8,128,2048]{2,1,0:T(8,128)(2,1)S(1)}, bf16[8,128,2048]{2,1,0:T(8,128)(2,1)}, u32[]{:S(2)}) %copy-start.1) | copy-done | bytes 4194328
  114.7 3.4 %shard_map.81.refs_0_ = bf16[4,512,256]{2,1,0:T(8,128)(2,1)} custom-call(s32[1]{0:T(128)} %bitcast.ids, bf16[1024,2048]{1,0:T(8,128)(2,1)S(1)} %bitcast.13, bf16[128,256]{1,0:T(8,128)(2,1)S(1)} %get-tuple-element.35.refs_0_, bf16[128,256]{1,0:T(8,128)(2,1)S(1)} %collective-permute-done.7.refs_1_, bf16[128,256]{1,0:T(8,128)(2,1)S(1)} %collective-permute-done.8.refs_2_, ...), custom_call_target="tpu_custom_call" | custom-call | flops 1073741824 | bytes 5767168 | tf_op jit(solution)/shard_map/pallas_call | solution.py:155
  118.3 23.0 %all_to_all.26 = bf16[32,64,128]{2,1,0:T(8,128)(2,1)S(1)} all-to-all(bf16[32,64,128]{2,1,0:T(8,128)(2,1)S(1)} %get-tuple-element.43.refs_0_), channel_id=1, replica_groups=mesh['seq'=32,'dp'=8] {'seq'}, dimensions={0} | all-to-all | bytes 1048576 | tf_op jit(solution)/shard_map/all_to_all | solution.py:189
  141.3 5.2 %reduce-scatter.2.cloned.1.call-done = bf16[512,256]{1,0:T(8,128)(2,1)} async-done(((bf16[2048,256]{1,0:T(8,128)(2,1)}), bf16[512,256]{1,0:T(8,128)(2,1)}) %reduce-scatter.2.cloned.1.call-update) | async-done | bytes 262160 | tf_op jit(solution)/shard_map/reduce_scatter | solution.py:245
  146.4 5.9 %all-to-all-start.4 = ((bf16[8,64,256]{2,1,0:T(8,128)(2,1)}), bf16[8,64,256]{2,1,0:T(8,128)(2,1)S(1)}, u32[]{:S(2)}, u32[]{:S(2)}) async-start(bf16[8,64,256]{2,1,0:T(8,128)(2,1)} %bitcast.31), calls=%async_computation.5 | async-start | bytes 524288 | tf_op jit(solution)/shard_map/all_to_all | solution.py:189
  154.4 3.0 %shard_map.83 = (bf16[128,2048]{1,0:T(8,128)(2,1)}, bf16[2048,128]{1,0:T(8,128)(2,1)S(1)}) custom-call(s32[1]{0:T(128)} %bitcast.ids, bf16[128,2048]{1,0:T(8,128)(2,1)S(1)} %bitcast.28, bf16[128,2048]{1,0:T(8,128)(2,1)S(1)} %bitcast.19, bf16[128,2048]{1,0:T(8,128)(2,1)S(1)} %copy-done.10, bf16[2048,128]{1,0:T(8,128)(2,1)S(1)} %bitcast.16, ...), custom_call_target="tpu_custom_call" | custom-call | flops 201326592 | bytes 3145728 | tf_op jit(solution)/shard_map/pallas_call | solution.py:155
  157.5 1.4 shard_map.84
  158.8 2.7 %all-to-all-done.4.part_ref = bf16[8,64,256]{2,1,0:T(8,128)(2,1)S(1)} async-done(((bf16[8,64,256]{2,1,0:T(8,128)(2,1)}), bf16[8,64,256]{2,1,0:T(8,128)(2,1)S(1)}, u32[]{:S(2)}, u32[]{:S(2)}) %all-to-all-start.4) | async-done | bytes 262176 | tf_op jit(solution)/shard_map/all_to_all | solution.py:189
  161.6 16.3 %all-gather = bf16[512,256]{1,0:T(8,128)(2,1)S(1)} all-gather(bf16[64,256]{1,0:T(8,128)(2,1)S(1)} %shard_map.85), channel_id=2, replica_groups=mesh['seq'=32,'dp'=8] {'dp'}, dimensions={0}, use_global_device_ids=true | all-gather | bytes 294912 | tf_op jit(solution)/shard_map/all_gather | solution.py:254
  (54 shorter events, 19.1 us)
Async XLA Ops:
  7.2 61.6 %all-gather.3.cloned.1.call-start = ((), (), s32[]{:S(2)}) async-start(), calls=%async_computation.6 | async-start | bytes 4718592 | tf_op jit(solution)/shard_map/all_gather | solution.py:203
  60.7 22.1 %all-to-all-start.1 = ((bf16[32,64,128]{2,1,0:T(8,128)(2,1)}), bf16[32,64,128]{2,1,0:T(8,128)(2,1)S(1)}, u32[]{:S(2)}, u32[]{:S(2)}) async-start(bf16[32,64,128]{2,1,0:T(8,128)(2,1)} %shard_map.77.refs_0_), calls=%async_computation.1 | async-start | bytes 1048576 | tf_op jit(solution)/shard_map/all_to_all | solution.py:189
  68.8 2.2 %copy-start = (bf16[8,128,2048]{2,1,0:T(8,128)(2,1)S(1)}, bf16[8,128,2048]{2,1,0:T(8,128)(2,1)}, u32[]{:S(2)}) copy-start(bf16[8,128,2048]{2,1,0:T(8,128)(2,1)} %all-gather.3.cloned.1.call-done.x_ref) | copy-start | bytes 12582916
  71.0 16.5 %copy-start.4 = (bf16[1,128,2048]{2,1,0:T(8,128)(2,1)S(1)}, bf16[1,128,2048]{2,1,0:T(8,128)(2,1)}, u32[]{:S(2)}) copy-start(bf16[1,128,2048]{2,1,0:T(8,128)(2,1)} %param.7) | copy-start | bytes 1572868
  73.0 26.0 %copy-start.3 = (bf16[1,128,2048]{2,1,0:T(8,128)(2,1)S(1)}, bf16[1,128,2048]{2,1,0:T(8,128)(2,1)}, u32[]{:S(2)}) copy-start(bf16[1,128,2048]{2,1,0:T(8,128)(2,1)} %param.8) | copy-start | bytes 1572868
  73.0 26.0 %copy-start.6 = (bf16[1,128,2048]{2,1,0:T(8,128)(2,1)S(1)}, bf16[1,128,2048]{2,1,0:T(8,128)(2,1)}, u32[]{:S(2)}) copy-start(bf16[1,128,2048]{2,1,0:T(8,128)(2,1)} %param.6) | copy-start | bytes 1572868
  73.1 6.3 %collective-permute-start = (bf16[128,256]{1,0:T(8,128)(2,1)S(1)}, bf16[128,256]{1,0:T(8,128)(2,1)S(1)}, u32[]{:S(2)}, u32[]{:S(2)}) collective-permute-start(bf16[128,256]{1,0:T(8,128)(2,1)S(1)} %get-tuple-element.26), channel_id=1, source_target_pairs={{0,1},{1,0},{2,3},{3,2},{4,5},{5,4},{6,7},{7,6},{8,9},{9,8},{10,11... | collective-permute-start | bytes 196616 | tf_op jit(solution)/shard_map/ppermute | solution.py:193
  74.3 7.5 %collective-permute-start.1 = (bf16[128,256]{1,0:T(8,128)(2,1)S(1)}, bf16[128,256]{1,0:T(8,128)(2,1)S(1)}, u32[]{:S(2)}, u32[]{:S(2)}) collective-permute-start(bf16[128,256]{1,0:T(8,128)(2,1)S(1)} %get-tuple-element.27), channel_id=1, source_target_pairs={{0,2},{1,3},{2,0},{3,1},{4,6},{5,7},{6,4},{7,5},{8,10},{9,11},{10,... | collective-permute-start | bytes 196616 | tf_op jit(solution)/shard_map/ppermute | solution.py:193
  75.5 7.3 %collective-permute-start.2 = (bf16[128,256]{1,0:T(8,128)(2,1)S(1)}, bf16[128,256]{1,0:T(8,128)(2,1)S(1)}, u32[]{:S(2)}, u32[]{:S(2)}) collective-permute-start(bf16[128,256]{1,0:T(8,128)(2,1)S(1)} %get-tuple-element.28), channel_id=1, source_target_pairs={{0,3},{1,2},{2,1},{3,0},{4,7},{5,6},{6,5},{7,4},{8,11},{9,10},{10,... | collective-permute-start | bytes 196616 | tf_op jit(solution)/shard_map/ppermute | solution.py:193
  76.0 6.9 %collective-permute-start.3 = (bf16[128,256]{1,0:T(8,128)(2,1)S(1)}, bf16[128,256]{1,0:T(8,128)(2,1)S(1)}, u32[]{:S(2)}, u32[]{:S(2)}) collective-permute-start(bf16[128,256]{1,0:T(8,128)(2,1)S(1)} %get-tuple-element.29), channel_id=1, source_target_pairs={{0,4},{1,5},{2,6},{3,7},{4,0},{5,1},{6,2},{7,3},{8,12},{9,13},{10,... | collective-permute-start | bytes 196616 | tf_op jit(solution)/shard_map/ppermute | solution.py:193
  78.8 6.1 %collective-permute-start.4 = (bf16[128,256]{1,0:T(8,128)(2,1)S(1)}, bf16[128,256]{1,0:T(8,128)(2,1)S(1)}, u32[]{:S(2)}, u32[]{:S(2)}) collective-permute-start(bf16[128,256]{1,0:T(8,128)(2,1)S(1)} %get-tuple-element.30), channel_id=1, source_target_pairs={{0,5},{1,4},{2,7},{3,6},{4,1},{5,0},{6,3},{7,2},{8,13},{9,12},{10,... | collective-permute-start | bytes 196616 | tf_op jit(solution)/shard_map/ppermute | solution.py:193
  79.3 6.9 %collective-permute-start.5 = (bf16[128,256]{1,0:T(8,128)(2,1)S(1)}, bf16[128,256]{1,0:T(8,128)(2,1)S(1)}, u32[]{:S(2)}, u32[]{:S(2)}) collective-permute-start(bf16[128,256]{1,0:T(8,128)(2,1)S(1)} %get-tuple-element.31), channel_id=1, source_target_pairs={{0,6},{1,7},{2,4},{3,5},{4,2},{5,3},{6,0},{7,1},{8,14},{9,15},{10,... | collective-permute-start | bytes 196616 | tf_op jit(solution)/shard_map/ppermute | solution.py:193
  81.8 5.7 %collective-permute-start.6 = (bf16[128,256]{1,0:T(8,128)(2,1)S(1)}, bf16[128,256]{1,0:T(8,128)(2,1)S(1)}, u32[]{:S(2)}, u32[]{:S(2)}) collective-permute-start(bf16[128,256]{1,0:T(8,128)(2,1)S(1)} %get-tuple-element.32), channel_id=1, source_target_pairs={{0,7},{1,6},{2,5},{3,4},{4,3},{5,2},{6,1},{7,0},{8,15},{9,14},{10,... | collective-permute-start | bytes 196616 | tf_op jit(solution)/shard_map/ppermute | solution.py:193
  89.5 28.7 %all-to-all-start.2 = ((bf16[32,64,128]{2,1,0:T(8,128)(2,1)}), bf16[32,64,128]{2,1,0:T(8,128)(2,1)S(1)}, u32[]{:S(2)}, u32[]{:S(2)}) async-start(bf16[32,64,128]{2,1,0:T(8,128)(2,1)} %bitcast.5), calls=%async_computation.2 | async-start | bytes 1048576 | tf_op jit(solution)/shard_map/all_to_all | solution.py:189
  99.0 47.4 %reduce-scatter.2.cloned.1.call-start = ((), (), s32[]{:S(2)}) async-start(), calls=%async_computation.7 | async-start | bytes 1310720 | tf_op jit(solution)/shard_map/reduce_scatter | solution.py:245
  100.0 7.0 %collective-permute-start.10 = (bf16[128,256]{1,0:T(8,128)(2,1)S(1)}, bf16[128,256]{1,0:T(8,128)(2,1)S(1)}, u32[]{:S(2)}, u32[]{:S(2)}) collective-permute-start(bf16[128,256]{1,0:T(8,128)(2,1)S(1)} %get-tuple-element.39), channel_id=1, source_target_pairs={{0,4},{1,5},{2,6},{3,7},{4,0},{5,1},{6,2},{7,3},{8,12},{9,13},{10,... | collective-permute-start | bytes 196616 | tf_op jit(solution)/shard_map/ppermute | solution.py:193
  101.2 6.4 %collective-permute-start.11 = (bf16[128,256]{1,0:T(8,128)(2,1)S(1)}, bf16[128,256]{1,0:T(8,128)(2,1)S(1)}, u32[]{:S(2)}, u32[]{:S(2)}) collective-permute-start(bf16[128,256]{1,0:T(8,128)(2,1)S(1)} %get-tuple-element.40), channel_id=1, source_target_pairs={{0,5},{1,4},{2,7},{3,6},{4,1},{5,0},{6,3},{7,2},{8,13},{9,12},{10,... | collective-permute-start | bytes 196616 | tf_op jit(solution)/shard_map/ppermute | solution.py:193
  103.9 5.3 %collective-permute-start.12 = (bf16[128,256]{1,0:T(8,128)(2,1)S(1)}, bf16[128,256]{1,0:T(8,128)(2,1)S(1)}, u32[]{:S(2)}, u32[]{:S(2)}) collective-permute-start(bf16[128,256]{1,0:T(8,128)(2,1)S(1)} %get-tuple-element.41), channel_id=1, source_target_pairs={{0,6},{1,7},{2,4},{3,5},{4,2},{5,3},{6,0},{7,1},{8,14},{9,15},{10,... | collective-permute-start | bytes 196616 | tf_op jit(solution)/shard_map/ppermute | solution.py:193
  104.5 6.2 %collective-permute-start.13 = (bf16[128,256]{1,0:T(8,128)(2,1)S(1)}, bf16[128,256]{1,0:T(8,128)(2,1)S(1)}, u32[]{:S(2)}, u32[]{:S(2)}) collective-permute-start(bf16[128,256]{1,0:T(8,128)(2,1)S(1)} %get-tuple-element.42), channel_id=1, source_target_pairs={{0,7},{1,6},{2,5},{3,4},{4,3},{5,2},{6,1},{7,0},{8,15},{9,14},{10,... | collective-permute-start | bytes 196616 | tf_op jit(solution)/shard_map/ppermute | solution.py:193
  106.3 4.3 %collective-permute-start.7 = (bf16[128,256]{1,0:T(8,128)(2,1)S(1)}, bf16[128,256]{1,0:T(8,128)(2,1)S(1)}, u32[]{:S(2)}, u32[]{:S(2)}) collective-permute-start(bf16[128,256]{1,0:T(8,128)(2,1)S(1)} %get-tuple-element.36), channel_id=1, source_target_pairs={{0,1},{1,0},{2,3},{3,2},{4,5},{5,4},{6,7},{7,6},{8,9},{9,8},{10,11... | collective-permute-start | bytes 196616 | tf_op jit(solution)/shard_map/ppermute | solution.py:193
  107.0 3.7 %collective-permute-start.8 = (bf16[128,256]{1,0:T(8,128)(2,1)S(1)}, bf16[128,256]{1,0:T(8,128)(2,1)S(1)}, u32[]{:S(2)}, u32[]{:S(2)}) collective-permute-start(bf16[128,256]{1,0:T(8,128)(2,1)S(1)} %get-tuple-element.37), channel_id=1, source_target_pairs={{0,2},{1,3},{2,0},{3,1},{4,6},{5,7},{6,4},{7,5},{8,10},{9,11},{10,... | collective-permute-start | bytes 196616 | tf_op jit(solution)/shard_map/ppermute | solution.py:193
  107.6 5.0 %collective-permute-start.9 = (bf16[128,256]{1,0:T(8,128)(2,1)S(1)}, bf16[128,256]{1,0:T(8,128)(2,1)S(1)}, u32[]{:S(2)}, u32[]{:S(2)}) collective-permute-start(bf16[128,256]{1,0:T(8,128)(2,1)S(1)} %get-tuple-element.38), channel_id=1, source_target_pairs={{0,3},{1,2},{2,1},{3,0},{4,7},{5,6},{6,5},{7,4},{8,11},{9,10},{10,... | collective-permute-start | bytes 196616 | tf_op jit(solution)/shard_map/ppermute | solution.py:193
  118.2 34.1 %copy-start.7 = (bf16[32,64,128]{2,1,0:T(8,128)(2,1)}, bf16[32,64,128]{2,1,0:T(8,128)(2,1)S(1)}, u32[]{:S(2)}) copy-start(bf16[32,64,128]{2,1,0:T(8,128)(2,1)S(1)} %get-tuple-element.43.refs_0_) | copy-start | bytes 1572868
  146.4 15.1 %all-to-all-start.4 = ((bf16[8,64,256]{2,1,0:T(8,128)(2,1)}), bf16[8,64,256]{2,1,0:T(8,128)(2,1)S(1)}, u32[]{:S(2)}, u32[]{:S(2)}) async-start(bf16[8,64,256]{2,1,0:T(8,128)(2,1)} %bitcast.31), calls=%async_computation.5 | async-start | bytes 524288 | tf_op jit(solution)/shard_map/all_to_all | solution.py:189
  (7 other events, 8.1 us)
Sparse Core Ops, SparseCore 0:
  9.9 38.8 all-gather.2
  118.4 28.0 reduce-scatter.1

commit v4 on v3

--- a/solution.py
+++ b/solution.py
@@ -32,16 +32,14 @@
     return t >= s
 
 
-def first_kernel(ids, q_ref, g_ref, w_ref, out_ref):
-    count, rows, _ = out_ref.shape
+def state_kernel(ids, q_ref, g_ref, *refs):
     for h in range(q_ref.shape[1] // HEAD):
-        state = dot(q_ref[:, cols(h)], g_ref[:, cols(h)], 0, 0).astype(BF16)
-        for i in range(HEAD // rows):
-            out_ref[h * (HEAD // rows) + i, :, :HEAD] = state[i * rows:(i + 1) * rows, :]
-    block = out_ref.shape[2] - HEAD
-    own = w_ref[:, span(ids[0], block)]
-    for i in range(count):
-        out_ref[i, :, HEAD:] = own
+        refs[-1][cols(h), :] = dot(q_ref[:, cols(h)], g_ref[:, cols(h)], 0, 0).astype(BF16)
+
+
+def plane_kernel(ids, *refs):
+    for o, ref in enumerate(refs[:-1]):
+        refs[-1][span(ids[2] ^ o, ref.shape[0]), :] = ref[...]
 
 
 def slot_state_kernel(slots, ids, left_ref, *refs):
@@ -66,16 +64,15 @@
         total = total + part_ref[i, :, :HEAD].astype(F32)
 
 
-def values_kernel(slots, ids, x_ref, first_ref, *refs):
-    outs, (w_ref, res_ref) = refs[-slots - 2:-2], refs[-2:]
+def values_kernel(slots, planes, ids, x_ref, *refs):
+    pieces, outs, (w_ref, res_ref) = refs[:planes], refs[-slots - 2:-2], refs[-2:]
     step = pl.program_id(0)
     count, rows = x_ref.shape[:2]
 
     @pl.when(step == 0)
     def _():
-        size = first_ref.shape[1]
-        for i in range(first_ref.shape[0]):
-            w_ref[i * size:(i + 1) * size, :] = first_ref[i, :, HEAD:]
+        for o, piece in enumerate(pieces):
+            w_ref[span(ids[1] ^ o, piece.shape[0]), :] = piece[...]
 
     x = x_ref[...].reshape(count * rows, x_ref.shape[2])
     res_ref[...] = dot(x, w_ref[...], 1, 0).astype(BF16).reshape(res_ref.shape)
@@ -182,35 +179,43 @@
     block = width_all // dp
     q, k, g = query_rows[0], key_rows[0], cotangent[0]
     head_flops = 2 * rows * HEAD * HEAD * heads
-    ids = lax.axis_index("dp").astype(jnp.int32)[None]
+    at_dp, at_seq = lax.axis_index("dp"), lax.axis_index("seq")
+    ids = jnp.stack([at_dp, at_seq // Z, at_seq % Z]).astype(jnp.int32)
 
 
     def exchange(array, groups=None):
         return lax.all_to_all(array, "seq", 0, 0, axis_index_groups=groups, tiled=True)
 
-    def swap_slots(arrays):
+    def swap_slots(arrays, axis="dp", stride=1):
+        count = lax.axis_size(axis)
         return [
-            a if o == 0 else lax.ppermute(a, "dp", [(i, i ^ o) for i in range(dp)])
+            a if o == 0 else lax.ppermute(a, axis, [(i, i ^ (o * stride)) for i in range(count)])
             for o, a in enumerate(arrays)
         ]
 
-    def sums_of(parts, reverse, through=()):
+    def sums_of(parts, reverse, through=(), after=()):
         return call(
             functools.partial(prefix_kernel, reverse), [((seq, width_all // seq, HEAD), BF16)],
-            seq * width_all // seq * HEAD, ids, parts, through=through,
+            seq * width_all // seq * HEAD, ids, parts, through=through, after=after,
         )
 
     all_inputs = lax.all_gather(inputs, "dp", axis=0, tiled=True)
 
-    first = exchange(call(
-        first_kernel, [((seq, width // seq, HEAD + block), BF16)], head_flops, ids, q, g, w_value
-    ))
-    qg_sums = sums_of(first, True)
+    own = lax.dynamic_slice_in_dim(w_value, at_dp * block, block, 1)
+    plane = call(
+        plane_kernel, [((Z * own.shape[0], block), BF16)], 0, ids, *swap_slots([own] * Z, "seq")
+    )
+    pieces = swap_slots([plane] * y_count, "seq", Z)
+    qg_local = call(
+        state_kernel, [((width_all, HEAD), BF16)], head_flops, ids, q, g, after=(plane,)
+    )
+    qg_parts = exchange(qg_local.reshape(seq, -1, HEAD))
+    qg_sums = sums_of(qg_parts, True, after=tuple(pieces[1:]))
     qg_round = exchange(qg_sums).reshape(width_all, HEAD)
 
     values = call(
-        functools.partial(values_kernel, dp), [((rows, block), BF16)] * dp,
-        2 * rows * width * width_all, ids, all_inputs, first, after=(qg_sums,),
+        functools.partial(values_kernel, dp, y_count), [((rows, block), BF16)] * dp,
+        2 * rows * width * width_all, ids, all_inputs, *pieces, after=(qg_sums,),
         grid=(dp // 2,),
         first=pl.BlockSpec((2, rows, width), lambda i, ids: ((ids[0] // 2) ^ i, 0, 0)),
         scratch=[pltpu.VMEM((width, block), BF16), pltpu.VMEM((2, rows, block), BF16)],

time: 186 us -> 193 us (1.038)
  blocking collectives: 87.8 us -> 40 us
  starting transfers between devices: 40.8 us -> 69.5 us
  waiting for transfers between devices: 18.3 us -> 35.3 us
  Pallas kernels: 14.2 us -> 23.1 us
    all_to_all x2 -> x1, blocking collectives: 71.5 us -> 23 us  [exchange(): lax.all_to_all(array, 'seq', 0, 0, axis_index_groups=groups, tiled=True)]
    ppermute x14 -> x24, starting transfers between devices: 17.2 us -> 37.6 us  [swap_slots(): lax.ppermute(a, axis, [(i, i ^ o * stride) for i in range(count)])]
    ppermute x14 -> x24, waiting for transfers between devices: 9.14 us -> 27.4 us  [swap_slots(): lax.ppermute(a, axis, [(i, i ^ o * stride) for i in range(count)])]
    pallas_call x11 -> x12, Pallas kernels: 14.2 us -> 23.1 us  [call(): pl.pallas_call(kernel, out_shape=[jax.ShapeDtypeStruct(x.shape, x.dtype)...]
    all_to_all x3 -> x4, starting transfers between devices: 23.5 us -> 31.8 us  [exchange(): lax.all_to_all(array, 'seq', 0, 0, axis_index_groups=groups, tiled=True)]
  transfers between devices with their start and end apart: 19 -> 30, of which waited for: 12 -> 12; matrix products, arithmetic and copies ran while one was open for 0% -> 0% of each run, Pallas kernels for 7% -> 9%
where the time goes in v4:
time: 193 us; the launch traced here: 192 us
  starting transfers between devices  69.5 us (36%)
  blocking collectives  40 us (21%)
  waiting for transfers between devices  35.3 us (18%)
  Pallas kernels  23.1 us (12%)
  between operations  14.2 us (7%)
  local copies, waits for them, and re-layouts  9.57 us (5%)
    ppermute x24, starting transfers between devices, swap_slots(): lax.ppermute(a, axis, [(i, i ^ o * stride) for i in range(count)])  37.6 us
    all_to_all x4, starting transfers between devices, exchange(): lax.all_to_all(array, 'seq', 0, 0, axis_index_groups=groups, tiled=True)  31.8 us
    ppermute x24, waiting for transfers between devices, swap_slots(): lax.ppermute(a, axis, [(i, i ^ o * stride) for i in range(count)])  27.4 us
    pallas_call x12, Pallas kernels, call(): pl.pallas_call(kernel, out_shape=[jax.ShapeDtypeStruct(x.shape, x.dtype)...  23.1 us
    all_to_all x1, blocking collectives, exchange(): lax.all_to_all(array, 'seq', 0, 0, axis_index_groups=groups, tiled=True)  23 us
    all_gather x1, blocking collectives, on_device(): lax.all_gather(summed, 'dp')  17 us
    unnamed x24, local copies, waits for them, and re-layouts  9.56 us
    reduce_scatter x1, waiting for transfers between devices, on_device(): lax.psum_scatter(terms.reshape(width, block), 'seq', scatter_dimension=0,...  5.42 us
  transfers between devices with their start and end apart: 30, of which 12 were waited for; matrix products, arithmetic and copies ran while one was open for 0% of the time, Pallas kernels for 9%

profile of v4, /device:TPU:1, one launch (start us, length us, event | category | flops | bytes accessed | tf_op | source)
XLA Modules:
  0.0 191.8 jit_solution(5241406412371779645)
XLA Ops:
  8.1 6.4 %collective-permute-start.6 = (bf16[64,256]{1,0:T(8,128)(2,1)S(1)}, bf16[64,256]{1,0:T(8,128)(2,1)S(1)}, u32[]{:S(2)}, u32[]{:S(2)}) collective-permute-start(bf16[64,256]{1,0:T(8,128)(2,1)S(1)} %constant_dynamic-slice_fusion.refs_0_), channel_id=1, source_target_pairs={{0,56},{8,48},{16,40},{24,32},{32,24},{40,16},{48,8},{56,0},{64,12... | collective-permute-start | bytes 98312 | tf_op jit(solution)/shard_map/ppermute | solution.py:192
  15.1 3.5 %collective-permute-start.4 = (bf16[64,256]{1,0:T(8,128)(2,1)S(1)}, bf16[64,256]{1,0:T(8,128)(2,1)S(1)}, u32[]{:S(2)}, u32[]{:S(2)}) collective-permute-start(bf16[64,256]{1,0:T(8,128)(2,1)S(1)} %constant_dynamic-slice_fusion.refs_0_), channel_id=1, source_target_pairs={{0,40},{8,32},{16,56},{24,48},{32,8},{40,0},{48,24},{56,16},{64,10... | collective-permute-start | bytes 98312 | tf_op jit(solution)/shard_map/ppermute | solution.py:192
  22.0 1.9 collective-permute-start
  31.0 7.6 %all-to-all-start = ((bf16[32,64,128]{2,1,0:T(8,128)(2,1)}), bf16[32,64,128]{2,1,0:T(8,128)(2,1)S(1)}, u32[]{:S(2)}, u32[]{:S(2)}) async-start(bf16[32,64,128]{2,1,0:T(8,128)(2,1)} %bitcast.6), calls=%async_computation | async-start | bytes 1048576 | tf_op jit(solution)/shard_map/all_to_all | solution.py:187
  38.6 2.6 %collective-permute-start.9 = (bf16[512,256]{1,0:T(8,128)(2,1)S(1)}, bf16[512,256]{1,0:T(8,128)(2,1)S(1)}, u32[]{:S(2)}, u32[]{:S(2)}) collective-permute-start(bf16[512,256]{1,0:T(8,128)(2,1)S(1)} %shard_map.76.refs_0_), channel_id=1, source_target_pairs={{0,192},{8,200},{16,208},{24,216},{32,224},{40,232},{48,240},{56,2... | collective-permute-start | bytes 786440 | tf_op jit(solution)/shard_map/ppermute | solution.py:192
  41.9 15.6 %collective-permute-done.9.refs_2_.refs_3_ = bf16[512,256]{1,0:T(8,128)(2,1)S(1)} collective-permute-done((bf16[512,256]{1,0:T(8,128)(2,1)S(1)}, bf16[512,256]{1,0:T(8,128)(2,1)S(1)}, u32[]{:S(2)}, u32[]{:S(2)}) %collective-permute-start.9) | collective-permute-done | bytes 262176 | tf_op jit(solution)/shard_map/ppermute | solution.py:192
  59.0 9.0 %all-to-all-start.1 = ((bf16[32,64,128]{2,1,0:T(8,128)(2,1)}), bf16[32,64,128]{2,1,0:T(8,128)(2,1)S(1)}, u32[]{:S(2)}, u32[]{:S(2)}) async-start(bf16[32,64,128]{2,1,0:T(8,128)(2,1)} %shard_map.78.refs_4_), calls=%async_computation.1 | async-start | bytes 1048576 | tf_op jit(solution)/shard_map/all_to_all | solution.py:187
  68.1 2.2 %copy-done.1 = bf16[8,128,2048]{2,1,0:T(8,128)(2,1)S(1)} copy-done((bf16[8,128,2048]{2,1,0:T(8,128)(2,1)S(1)}, bf16[8,128,2048]{2,1,0:T(8,128)(2,1)}, u32[]{:S(2)}) %copy-start.1) | copy-done | bytes 4194328
  70.2 3.3 %shard_map.79 = (bf16[128,256]{1,0:T(8,128)(2,1)S(1)}, bf16[128,256]{1,0:T(8,128)(2,1)S(1)}, bf16[128,256]{1,0:T(8,128)(2,1)S(1)}, bf16[128,256]{1,0:T(8,128)(2,...) custom-call(s32[3]{0:T(128)S(1)} %pad_add_fusion.ids, ...), custom_call_target="tpu_custom_call" | custom-call | flops 1073741824 | bytes 5767168 | tf_op jit(solution)/shard_map/pallas_call | solution.py:152
  73.6 1.9 %collective-permute-start.10 = (bf16[128,256]{1,0:T(8,128)(2,1)S(1)}, bf16[128,256]{1,0:T(8,128)(2,1)S(1)}, u32[]{:S(2)}, u32[]{:S(2)}) collective-permute-start(bf16[128,256]{1,0:T(8,128)(2,1)S(1)} %get-tuple-element.26), channel_id=1, source_target_pairs={{0,1},{1,0},{2,3},{3,2},{4,5},{5,4},{6,7},{7,6},{8,9},{9,8},{10,11... | collective-permute-start | bytes 196616 | tf_op jit(solution)/shard_map/ppermute | solution.py:192
  77.1 2.7 %collective-permute-start.13 = (bf16[128,256]{1,0:T(8,128)(2,1)}, bf16[128,256]{1,0:T(8,128)(2,1)S(1)}, u32[]{:S(2)}, u32[]{:S(2)}) collective-permute-start(bf16[128,256]{1,0:T(8,128)(2,1)} %get-tuple-element.29), channel_id=1, source_target_pairs={{0,4},{1,5},{2,6},{3,7},{4,0},{5,1},{6,2},{7,3},{8,12},{9,13},{10,... | collective-permute-start | bytes 196616 | tf_op jit(solution)/shard_map/ppermute | solution.py:192
  80.5 2.5 %collective-permute-start.15 = (bf16[128,256]{1,0:T(8,128)(2,1)}, bf16[128,256]{1,0:T(8,128)(2,1)S(1)}, u32[]{:S(2)}, u32[]{:S(2)}) collective-permute-start(bf16[128,256]{1,0:T(8,128)(2,1)} %get-tuple-element.31), channel_id=1, source_target_pairs={{0,6},{1,7},{2,4},{3,5},{4,2},{5,3},{6,0},{7,1},{8,14},{9,15},{10,... | collective-permute-start | bytes 196616 | tf_op jit(solution)/shard_map/ppermute | solution.py:192
  91.2 9.5 %all-to-all-start.2 = ((bf16[32,64,128]{2,1,0:T(8,128)(2,1)}), bf16[32,64,128]{2,1,0:T(8,128)(2,1)S(1)}, u32[]{:S(2)}, u32[]{:S(2)}) async-start(bf16[32,64,128]{2,1,0:T(8,128)(2,1)} %bitcast.8), calls=%async_computation.2 | async-start | bytes 1048576 | tf_op jit(solution)/shard_map/all_to_all | solution.py:187
  105.9 2.1 %collective-permute-start.21 = (bf16[128,256]{1,0:T(8,128)(2,1)S(1)}, bf16[128,256]{1,0:T(8,128)(2,1)S(1)}, u32[]{:S(2)}, u32[]{:S(2)}) collective-permute-start(bf16[128,256]{1,0:T(8,128)(2,1)S(1)} %get-tuple-element.40), channel_id=1, source_target_pairs={{0,5},{1,4},{2,7},{3,6},{4,1},{5,0},{6,3},{7,2},{8,13},{9,12},{10,... | collective-permute-start | bytes 196616 | tf_op jit(solution)/shard_map/ppermute | solution.py:192
  108.9 2.1 %collective-permute-start.23 = (bf16[128,256]{1,0:T(8,128)(2,1)S(1)}, bf16[128,256]{1,0:T(8,128)(2,1)S(1)}, u32[]{:S(2)}, u32[]{:S(2)}) collective-permute-start(bf16[128,256]{1,0:T(8,128)(2,1)S(1)} %get-tuple-element.42), channel_id=1, source_target_pairs={{0,7},{1,6},{2,5},{3,4},{4,3},{5,2},{6,1},{7,0},{8,15},{9,14},{10,... | collective-permute-start | bytes 196616 | tf_op jit(solution)/shard_map/ppermute | solution.py:192
  112.9 1.9 collective-permute-done.23.refs_7_
  114.8 2.2 %copy-done.2 = bf16[8,128,2048]{2,1,0:T(8,128)(2,1)S(1)} copy-done((bf16[8,128,2048]{2,1,0:T(8,128)(2,1)S(1)}, bf16[8,128,2048]{2,1,0:T(8,128)(2,1)}, u32[]{:S(2)}) %copy-start.2) | copy-done | bytes 4194328
  117.0 4.0 %shard_map.82.refs_0_ = bf16[4,512,256]{2,1,0:T(8,128)(2,1)} custom-call(s32[3]{0:T(128)S(1)} %pad_add_fusion.ids, bf16[1024,2048]{1,0:T(8,128)(2,1)S(1)} %bitcast.16, bf16[128,256]{1,0:T(8,128)(2,1)S(1)} %get-tuple-element.35.refs_0_, bf16[128,256]{1,0:T(8,128)(2,1)S(1)} %collective-permute-done.17.refs_1_, ...), custom_call_target="tpu_custom_call" | custom-call | flops 1073741824 | bytes 5767168 | tf_op jit(solution)/shard_map/pallas_call | solution.py:152
  121.6 23.0 %all_to_all.25 = bf16[32,64,128]{2,1,0:T(8,128)(2,1)S(1)} all-to-all(bf16[32,64,128]{2,1,0:T(8,128)(2,1)S(1)} %get-tuple-element.43.refs_0_), channel_id=1, replica_groups=mesh['seq'=32,'dp'=8] {'seq'}, dimensions={0} | all-to-all | bytes 1048576 | tf_op jit(solution)/shard_map/all_to_all | solution.py:187
  144.6 5.4 %reduce-scatter.2.cloned.1.call-done = bf16[512,256]{1,0:T(8,128)(2,1)} async-done(((bf16[2048,256]{1,0:T(8,128)(2,1)}), bf16[512,256]{1,0:T(8,128)(2,1)}) %reduce-scatter.2.cloned.1.call-update) | async-done | bytes 262160 | tf_op jit(solution)/shard_map/reduce_scatter | solution.py:250
  150.1 5.7 %all-to-all-start.4 = ((bf16[8,64,256]{2,1,0:T(8,128)(2,1)}), bf16[8,64,256]{2,1,0:T(8,128)(2,1)}, u32[]{:S(2)}, u32[]{:S(2)}) async-start(bf16[8,64,256]{2,1,0:T(8,128)(2,1)} %bitcast.34), calls=%async_computation.5 | async-start | bytes 524288 | tf_op jit(solution)/shard_map/all_to_all | solution.py:187
  157.9 3.6 %shard_map.84 = (bf16[128,2048]{1,0:T(8,128)(2,1)}, bf16[2048,128]{1,0:T(8,128)(2,1)S(1)}) custom-call(s32[3]{0:T(128)S(1)} %pad_add_fusion.ids, bf16[128,2048]{1,0:T(8,128)(2,1)S(1)} %bitcast.31, bf16[128,2048]{1,0:T(8,128)(2,1)S(1)} %bitcast.22, bf16[128,2048]{1,0:T(8,128)(2,1)S(1)} %copy-done.11, bf16[2048,128]{1,0:T(8,128)(2,1)S(1)} %bitcast.19, ...), custom_call_target="tpu_custom_call" | custom-call | flops 201326592 | bytes 3145728 | tf_op jit(solution)/shard_map/pallas_call | solution.py:152
  161.4 1.9 shard_map.85
  166.6 17.0 %all-gather = bf16[512,256]{1,0:T(8,128)(2,1)S(1)} all-gather(bf16[64,256]{1,0:T(8,128)(2,1)S(1)} %shard_map.86), channel_id=2, replica_groups=mesh['seq'=32,'dp'=8] {'dp'}, dimensions={0}, use_global_device_ids=true | all-gather | bytes 294912 | tf_op jit(solution)/shard_map/all_gather | solution.py:259
  (78 shorter events, 40.0 us)
Async XLA Ops:
  7.2 60.9 %all-gather.3.cloned.1.call-start = ((), (), s32[]{:S(2)}) async-start(), calls=%async_computation.6 | async-start | bytes 4718592 | tf_op jit(solution)/shard_map/all_gather | solution.py:202
  8.1 13.9 %collective-permute-start.6 = (bf16[64,256]{1,0:T(8,128)(2,1)S(1)}, bf16[64,256]{1,0:T(8,128)(2,1)S(1)}, u32[]{:S(2)}, u32[]{:S(2)}) collective-permute-start(bf16[64,256]{1,0:T(8,128)(2,1)S(1)} %constant_dynamic-slice_fusion.refs_0_), channel_id=1, source_target_pairs={{0,56},{8,48},{16,40},{24,32},{32,24},{40,16},{48,8},{56,0},{64,12... | collective-permute-start | bytes 98312 | tf_op jit(solution)/shard_map/ppermute | solution.py:192
  14.5 7.5 %collective-permute-start.5 = (bf16[64,256]{1,0:T(8,128)(2,1)S(1)}, bf16[64,256]{1,0:T(8,128)(2,1)S(1)}, u32[]{:S(2)}, u32[]{:S(2)}) collective-permute-start(bf16[64,256]{1,0:T(8,128)(2,1)S(1)} %constant_dynamic-slice_fusion.refs_0_), channel_id=1, source_target_pairs={{0,48},{8,56},{16,32},{24,40},{32,16},{40,24},{48,0},{56,8},{64,11... | collective-permute-start | bytes 98312 | tf_op jit(solution)/shard_map/ppermute | solution.py:192
  15.1 8.9 %collective-permute-start.4 = (bf16[64,256]{1,0:T(8,128)(2,1)S(1)}, bf16[64,256]{1,0:T(8,128)(2,1)S(1)}, u32[]{:S(2)}, u32[]{:S(2)}) collective-permute-start(bf16[64,256]{1,0:T(8,128)(2,1)S(1)} %constant_dynamic-slice_fusion.refs_0_), channel_id=1, source_target_pairs={{0,40},{8,32},{16,56},{24,48},{32,8},{40,0},{48,24},{56,16},{64,10... | collective-permute-start | bytes 98312 | tf_op jit(solution)/shard_map/ppermute | solution.py:192
  18.5 7.0 %collective-permute-start.3 = (bf16[64,256]{1,0:T(8,128)(2,1)S(1)}, bf16[64,256]{1,0:T(8,128)(2,1)S(1)}, u32[]{:S(2)}, u32[]{:S(2)}) collective-permute-start(bf16[64,256]{1,0:T(8,128)(2,1)S(1)} %constant_dynamic-slice_fusion.refs_0_), channel_id=1, source_target_pairs={{0,32},{8,40},{16,48},{24,56},{32,0},{40,8},{48,16},{56,24},{64,96... | collective-permute-start | bytes 98312 | tf_op jit(solution)/shard_map/ppermute | solution.py:192
  31.0 26.6 %all-to-all-start = ((bf16[32,64,128]{2,1,0:T(8,128)(2,1)}), bf16[32,64,128]{2,1,0:T(8,128)(2,1)S(1)}, u32[]{:S(2)}, u32[]{:S(2)}) async-start(bf16[32,64,128]{2,1,0:T(8,128)(2,1)} %bitcast.6), calls=%async_computation | async-start | bytes 1048576 | tf_op jit(solution)/shard_map/all_to_all | solution.py:187
  38.6 19.0 %collective-permute-start.9 = (bf16[512,256]{1,0:T(8,128)(2,1)S(1)}, bf16[512,256]{1,0:T(8,128)(2,1)S(1)}, u32[]{:S(2)}, u32[]{:S(2)}) collective-permute-start(bf16[512,256]{1,0:T(8,128)(2,1)S(1)} %shard_map.76.refs_0_), channel_id=1, source_target_pairs={{0,192},{8,200},{16,208},{24,216},{32,224},{40,232},{48,240},{56,2... | collective-permute-start | bytes 786440 | tf_op jit(solution)/shard_map/ppermute | solution.py:192
  41.2 16.4 %collective-permute-start.8 = (bf16[512,256]{1,0:T(8,128)(2,1)S(1)}, bf16[512,256]{1,0:T(8,128)(2,1)S(1)}, u32[]{:S(2)}, u32[]{:S(2)}) collective-permute-start(bf16[512,256]{1,0:T(8,128)(2,1)S(1)} %shard_map.76.refs_0_), channel_id=1, source_target_pairs={{0,128},{8,136},{16,144},{24,152},{32,160},{40,168},{48,176},{56,1... | collective-permute-start | bytes 786440 | tf_op jit(solution)/shard_map/ppermute | solution.py:192
  41.7 15.9 %collective-permute-start.7 = (bf16[512,256]{1,0:T(8,128)(2,1)S(1)}, bf16[512,256]{1,0:T(8,128)(2,1)S(1)}, u32[]{:S(2)}, u32[]{:S(2)}) collective-permute-start(bf16[512,256]{1,0:T(8,128)(2,1)S(1)} %shard_map.76.refs_0_), channel_id=1, source_target_pairs={{0,64},{8,72},{16,80},{24,88},{32,96},{40,104},{48,112},{56,120},{... | collective-permute-start | bytes 786440 | tf_op jit(solution)/shard_map/ppermute | solution.py:192
  59.0 24.4 %all-to-all-start.1 = ((bf16[32,64,128]{2,1,0:T(8,128)(2,1)}), bf16[32,64,128]{2,1,0:T(8,128)(2,1)S(1)}, u32[]{:S(2)}, u32[]{:S(2)}) async-start(bf16[32,64,128]{2,1,0:T(8,128)(2,1)} %shard_map.78.refs_4_), calls=%async_computation.1 | async-start | bytes 1048576 | tf_op jit(solution)/shard_map/all_to_all | solution.py:187
  73.6 6.9 %collective-permute-start.10 = (bf16[128,256]{1,0:T(8,128)(2,1)S(1)}, bf16[128,256]{1,0:T(8,128)(2,1)S(1)}, u32[]{:S(2)}, u32[]{:S(2)}) collective-permute-start(bf16[128,256]{1,0:T(8,128)(2,1)S(1)} %get-tuple-element.26), channel_id=1, source_target_pairs={{0,1},{1,0},{2,3},{3,2},{4,5},{5,4},{6,7},{7,6},{8,9},{9,8},{10,11... | collective-permute-start | bytes 196616 | tf_op jit(solution)/shard_map/ppermute | solution.py:192
  75.5 7.5 %collective-permute-start.11 = (bf16[128,256]{1,0:T(8,128)(2,1)S(1)}, bf16[128,256]{1,0:T(8,128)(2,1)S(1)}, u32[]{:S(2)}, u32[]{:S(2)}) collective-permute-start(bf16[128,256]{1,0:T(8,128)(2,1)S(1)} %get-tuple-element.27), channel_id=1, source_target_pairs={{0,2},{1,3},{2,0},{3,1},{4,6},{5,7},{6,4},{7,5},{8,10},{9,11},{10,... | collective-permute-start | bytes 196616 | tf_op jit(solution)/shard_map/ppermute | solution.py:192
  76.7 6.6 %collective-permute-start.12 = (bf16[128,256]{1,0:T(8,128)(2,1)}, bf16[128,256]{1,0:T(8,128)(2,1)S(1)}, u32[]{:S(2)}, u32[]{:S(2)}) collective-permute-start(bf16[128,256]{1,0:T(8,128)(2,1)} %get-tuple-element.28), channel_id=1, source_target_pairs={{0,3},{1,2},{2,1},{3,0},{4,7},{5,6},{6,5},{7,4},{8,11},{9,10},{10,... | collective-permute-start | bytes 196616 | tf_op jit(solution)/shard_map/ppermute | solution.py:192
  77.1 7.1 %collective-permute-start.13 = (bf16[128,256]{1,0:T(8,128)(2,1)}, bf16[128,256]{1,0:T(8,128)(2,1)S(1)}, u32[]{:S(2)}, u32[]{:S(2)}) collective-permute-start(bf16[128,256]{1,0:T(8,128)(2,1)} %get-tuple-element.29), channel_id=1, source_target_pairs={{0,4},{1,5},{2,6},{3,7},{4,0},{5,1},{6,2},{7,3},{8,12},{9,13},{10,... | collective-permute-start | bytes 196616 | tf_op jit(solution)/shard_map/ppermute | solution.py:192
  79.9 6.1 %collective-permute-start.14 = (bf16[128,256]{1,0:T(8,128)(2,1)}, bf16[128,256]{1,0:T(8,128)(2,1)S(1)}, u32[]{:S(2)}, u32[]{:S(2)}) collective-permute-start(bf16[128,256]{1,0:T(8,128)(2,1)} %get-tuple-element.30), channel_id=1, source_target_pairs={{0,5},{1,4},{2,7},{3,6},{4,1},{5,0},{6,3},{7,2},{8,13},{9,12},{10,... | collective-permute-start | bytes 196616 | tf_op jit(solution)/shard_map/ppermute | solution.py:192
  80.5 6.8 %collective-permute-start.15 = (bf16[128,256]{1,0:T(8,128)(2,1)}, bf16[128,256]{1,0:T(8,128)(2,1)S(1)}, u32[]{:S(2)}, u32[]{:S(2)}) collective-permute-start(bf16[128,256]{1,0:T(8,128)(2,1)} %get-tuple-element.31), channel_id=1, source_target_pairs={{0,6},{1,7},{2,4},{3,5},{4,2},{5,3},{6,0},{7,1},{8,14},{9,15},{10,... | collective-permute-start | bytes 196616 | tf_op jit(solution)/shard_map/ppermute | solution.py:192
  91.2 29.8 %all-to-all-start.2 = ((bf16[32,64,128]{2,1,0:T(8,128)(2,1)}), bf16[32,64,128]{2,1,0:T(8,128)(2,1)S(1)}, u32[]{:S(2)}, u32[]{:S(2)}) async-start(bf16[32,64,128]{2,1,0:T(8,128)(2,1)} %bitcast.8), calls=%async_computation.2 | async-start | bytes 1048576 | tf_op jit(solution)/shard_map/all_to_all | solution.py:187
  100.7 49.4 %reduce-scatter.2.cloned.1.call-start = ((), (), s32[]{:S(2)}) async-start(), calls=%async_computation.7 | async-start | bytes 1310720 | tf_op jit(solution)/shard_map/reduce_scatter | solution.py:250
  103.0 5.9 %collective-permute-start.18 = (bf16[128,256]{1,0:T(8,128)(2,1)S(1)}, bf16[128,256]{1,0:T(8,128)(2,1)S(1)}, u32[]{:S(2)}, u32[]{:S(2)}) collective-permute-start(bf16[128,256]{1,0:T(8,128)(2,1)S(1)} %get-tuple-element.37), channel_id=1, source_target_pairs={{0,2},{1,3},{2,0},{3,1},{4,6},{5,7},{6,4},{7,5},{8,10},{9,11},{10,... | collective-permute-start | bytes 196616 | tf_op jit(solution)/shard_map/ppermute | solution.py:192
  103.0 7.9 %collective-permute-start.19 = (bf16[128,256]{1,0:T(8,128)(2,1)S(1)}, bf16[128,256]{1,0:T(8,128)(2,1)S(1)}, u32[]{:S(2)}, u32[]{:S(2)}) collective-permute-start(bf16[128,256]{1,0:T(8,128)(2,1)S(1)} %get-tuple-element.38), channel_id=1, source_target_pairs={{0,3},{1,2},{2,1},{3,0},{4,7},{5,6},{6,5},{7,4},{8,11},{9,10},{10,... | collective-permute-start | bytes 196616 | tf_op jit(solution)/shard_map/ppermute | solution.py:192
  104.7 6.2 %collective-permute-start.20 = (bf16[128,256]{1,0:T(8,128)(2,1)S(1)}, bf16[128,256]{1,0:T(8,128)(2,1)S(1)}, u32[]{:S(2)}, u32[]{:S(2)}) collective-permute-start(bf16[128,256]{1,0:T(8,128)(2,1)S(1)} %get-tuple-element.39), channel_id=1, source_target_pairs={{0,4},{1,5},{2,6},{3,7},{4,0},{5,1},{6,2},{7,3},{8,12},{9,13},{10,... | collective-permute-start | bytes 196616 | tf_op jit(solution)/shard_map/ppermute | solution.py:192
  105.9 6.0 %collective-permute-start.21 = (bf16[128,256]{1,0:T(8,128)(2,1)S(1)}, bf16[128,256]{1,0:T(8,128)(2,1)S(1)}, u32[]{:S(2)}, u32[]{:S(2)}) collective-permute-start(bf16[128,256]{1,0:T(8,128)(2,1)S(1)} %get-tuple-element.40), channel_id=1, source_target_pairs={{0,5},{1,4},{2,7},{3,6},{4,1},{5,0},{6,3},{7,2},{8,13},{9,12},{10,... | collective-permute-start | bytes 196616 | tf_op jit(solution)/shard_map/ppermute | solution.py:192
  108.9 5.9 %collective-permute-start.23 = (bf16[128,256]{1,0:T(8,128)(2,1)S(1)}, bf16[128,256]{1,0:T(8,128)(2,1)S(1)}, u32[]{:S(2)}, u32[]{:S(2)}) collective-permute-start(bf16[128,256]{1,0:T(8,128)(2,1)S(1)} %get-tuple-element.42), channel_id=1, source_target_pairs={{0,7},{1,6},{2,5},{3,4},{4,3},{5,2},{6,1},{7,0},{8,15},{9,14},{10,... | collective-permute-start | bytes 196616 | tf_op jit(solution)/shard_map/ppermute | solution.py:192
  150.1 15.0 %all-to-all-start.4 = ((bf16[8,64,256]{2,1,0:T(8,128)(2,1)}), bf16[8,64,256]{2,1,0:T(8,128)(2,1)}, u32[]{:S(2)}, u32[]{:S(2)}) async-start(bf16[8,64,256]{2,1,0:T(8,128)(2,1)} %bitcast.34), calls=%async_computation.5 | async-start | bytes 524288 | tf_op jit(solution)/shard_map/all_to_all | solution.py:187
  (18 other events, 186.4 us)
Sparse Core Ops, SparseCore 0:
  9.9 38.8 all-gather.2
  121.7 28.2 reduce-scatter.1

commit v5 on v3

--- a/solution.py
+++ b/solution.py
@@ -215,17 +215,17 @@
         first=pl.BlockSpec((2, rows, width), lambda i, ids: ((ids[0] // 2) ^ i, 0, 0)),
         scratch=[pltpu.VMEM((width, block), BF16), pltpu.VMEM((2, rows, block), BF16)],
     )
+    grad_values = call(
+        functools.partial(grad_values_kernel, scale, dp), [((rows, block), BF16)] * dp,
+        3 * head_flops, ids, q, k, g, qg_round,
+    )
     kv_local, values = call(
         functools.partial(slot_state_kernel, dp),
         [((heads * HEAD, HEAD), BF16), ((rows, width_all), BF16)], head_flops, ids, k,
-        *swap_slots(values), after=(qg_round,),
+        *swap_slots(values), after=(grad_values[0],),
     )
     kv_parts = exchange(kv_local.reshape(seq, -1, HEAD))
 
-    grad_values = call(
-        functools.partial(grad_values_kernel, scale, dp), [((rows, block), BF16)] * dp,
-        3 * head_flops, ids, q, k, g, qg_round, after=(kv_local,),
-    )
     terms = call(
         functools.partial(product_kernel, dp), [((y_count, width // y_count, block), BF16)],
         2 * rows * width * width_all, ids, all_inputs.reshape(dp * rows, width),

time: 186 us -> 186 us (level)
  waiting for transfers between devices: 18.3 us -> 15.5 us
    ppermute x14, waiting for transfers between devices: 9.14 us -> 6.47 us  [swap_slots(): lax.ppermute(a, 'dp', [(i, i ^ o) for i in range(dp)])]
    unnamed x24 -> x26, local copies, waits for them, and re-layouts: 10.3 us -> 11.3 us
  transfers between devices with their start and end apart: 19 -> 19, of which waited for: 12 -> 8; matrix products, arithmetic and copies ran while one was open for 0% -> 0% of each run, Pallas kernels for 7% -> 6%
where the time goes in v5:
time: 186 us
  blocking collectives  88.3 us (47%)
  starting transfers between devices  42.2 us (23%)
  waiting for transfers between devices  15.5 us (8%)
  Pallas kernels  14.2 us (8%)
  between operations  14.2 us (8%)
  local copies, waits for them, and re-layouts  11.3 us (6%)
    all_to_all x2, blocking collectives, exchange(): lax.all_to_all(array, 'seq', 0, 0, axis_index_groups=groups, tiled=True)  72.9 us
    all_to_all x3, starting transfers between devices, exchange(): lax.all_to_all(array, 'seq', 0, 0, axis_index_groups=groups, tiled=True)  24.2 us
    ppermute x14, starting transfers between devices, swap_slots(): lax.ppermute(a, 'dp', [(i, i ^ o) for i in range(dp)])  17.9 us
    all_gather x1, blocking collectives, on_device(): lax.all_gather(summed, 'dp')  15.4 us
    pallas_call x11, Pallas kernels, call(): pl.pallas_call(kernel, out_shape=[jax.ShapeDtypeStruct(x.shape, x.dtype)...  14.2 us
    unnamed x26, local copies, waits for them, and re-layouts  11.3 us
    ppermute x14, waiting for transfers between devices, swap_slots(): lax.ppermute(a, 'dp', [(i, i ^ o) for i in range(dp)])  6.47 us
    all_to_all x3, waiting for transfers between devices, exchange(): lax.all_to_all(array, 'seq', 0, 0, axis_index_groups=groups, tiled=True)  4.16 us
  transfers between devices with their start and end apart: 19, of which 8 were waited for; matrix products, arithmetic and copies ran while one was open for 0% of the time, Pallas kernels for 6%

profile of v5, /device:TPU:1, one launch (start us, length us, event | category | flops | bytes accessed | tf_op | source)
XLA Modules:
  0.0 185.6 jit_solution(2173593012844172813)
XLA Ops:
  11.3 48.5 %all_to_all.25.part_ref.first_ref = bf16[32,64,384]{2,1,0:T(8,128)(2,1)S(1)} all-to-all(bf16[32,64,384]{2,1,0:T(8,128)(2,1)S(1)} %shard_map.76), channel_id=1, replica_groups=mesh['seq'=32,'dp'=8] {'seq'}, dimensions={0} | all-to-all | bytes 3145728 | tf_op jit(solution)/shard_map/all_to_all | solution.py:189
  60.7 8.1 %all-to-all-start.1 = ((bf16[32,64,128]{2,1,0:T(8,128)(2,1)}), bf16[32,64,128]{2,1,0:T(8,128)(2,1)S(1)}, u32[]{:S(2)}, u32[]{:S(2)}) async-start(bf16[32,64,128]{2,1,0:T(8,128)(2,1)} %shard_map.77.refs_0_), calls=%async_computation.1 | async-start | bytes 1048576 | tf_op jit(solution)/shard_map/all_to_all | solution.py:189
  68.8 2.2 %copy-done = bf16[8,128,2048]{2,1,0:T(8,128)(2,1)S(1)} copy-done((bf16[8,128,2048]{2,1,0:T(8,128)(2,1)S(1)}, bf16[8,128,2048]{2,1,0:T(8,128)(2,1)}, u32[]{:S(2)}) %copy-start) | copy-done | bytes 4194328
  71.0 2.0 %shard_map.78 = (bf16[128,256]{1,0:T(8,128)(2,1)S(1)}, bf16[128,256]{1,0:T(8,128)(2,1)S(1)}, bf16[128,256]{1,0:T(8,128)(2,1)S(1)}, bf16[128,256]{1,0:T(8,128)(2,...) custom-call(s32[1]{0:T(128)} %bitcast.ids, ...), custom_call_target="tpu_custom_call" | custom-call | flops 1073741824 | bytes 6291456 | tf_op jit(solution)/shard_map/pallas_call | solution.py:155
  73.0 1.3 collective-permute-start
  74.3 1.2 collective-permute-start.1
  76.0 2.7 %collective-permute-start.3 = (bf16[128,256]{1,0:T(8,128)(2,1)S(1)}, bf16[128,256]{1,0:T(8,128)(2,1)S(1)}, u32[]{:S(2)}, u32[]{:S(2)}) collective-permute-start(bf16[128,256]{1,0:T(8,128)(2,1)S(1)} %get-tuple-element.29), channel_id=1, source_target_pairs={{0,4},{1,5},{2,6},{3,7},{4,0},{5,1},{6,2},{7,3},{8,12},{9,13},{10,... | collective-permute-start | bytes 196616 | tf_op jit(solution)/shard_map/ppermute | solution.py:193
  79.3 2.5 %collective-permute-start.5 = (bf16[128,256]{1,0:T(8,128)(2,1)S(1)}, bf16[128,256]{1,0:T(8,128)(2,1)S(1)}, u32[]{:S(2)}, u32[]{:S(2)}) collective-permute-start(bf16[128,256]{1,0:T(8,128)(2,1)S(1)} %get-tuple-element.31), channel_id=1, source_target_pairs={{0,6},{1,7},{2,4},{3,5},{4,2},{5,3},{6,0},{7,1},{8,14},{9,15},{10,... | collective-permute-start | bytes 196616 | tf_op jit(solution)/shard_map/ppermute | solution.py:193
  84.9 1.3 collective-permute-done.5.refs_6_
  86.2 1.3 collective-permute-done.6.refs_7_
  89.5 9.5 %all-to-all-start.2 = ((bf16[32,64,128]{2,1,0:T(8,128)(2,1)}), bf16[32,64,128]{2,1,0:T(8,128)(2,1)S(1)}, u32[]{:S(2)}, u32[]{:S(2)}) async-start(bf16[32,64,128]{2,1,0:T(8,128)(2,1)} %bitcast.5), calls=%async_computation.2 | async-start | bytes 1048576 | tf_op jit(solution)/shard_map/all_to_all | solution.py:189
  99.8 1.7 collective-permute-start.9
  102.6 2.3 %collective-permute-start.11 = (bf16[128,256]{1,0:T(8,128)(2,1)S(1)}, bf16[128,256]{1,0:T(8,128)(2,1)S(1)}, u32[]{:S(2)}, u32[]{:S(2)}) collective-permute-start(bf16[128,256]{1,0:T(8,128)(2,1)S(1)} %get-tuple-element.40), channel_id=1, source_target_pairs={{0,5},{1,4},{2,7},{3,6},{4,1},{5,0},{6,3},{7,2},{8,13},{9,12},{10,... | collective-permute-start | bytes 196616 | tf_op jit(solution)/shard_map/ppermute | solution.py:193
  105.4 2.3 %collective-permute-start.13 = (bf16[128,256]{1,0:T(8,128)(2,1)S(1)}, bf16[128,256]{1,0:T(8,128)(2,1)S(1)}, u32[]{:S(2)}, u32[]{:S(2)}) collective-permute-start(bf16[128,256]{1,0:T(8,128)(2,1)S(1)} %get-tuple-element.42), channel_id=1, source_target_pairs={{0,7},{1,6},{2,5},{3,4},{4,3},{5,2},{6,1},{7,0},{8,15},{9,14},{10,... | collective-permute-start | bytes 196616 | tf_op jit(solution)/shard_map/ppermute | solution.py:193
  109.7 1.9 %collective-permute-done.13.refs_7_ = bf16[128,256]{1,0:T(8,128)(2,1)S(1)} collective-permute-done((bf16[128,256]{1,0:T(8,128)(2,1)S(1)}, bf16[128,256]{1,0:T(8,128)(2,1)S(1)}, u32[]{:S(2)}, u32[]{:S(2)}) %collective-permute-start.13) | collective-permute-done | bytes 65568 | tf_op jit(solution)/shard_map/ppermute | solution.py:193
  111.5 2.2 %copy-done.1 = bf16[8,128,2048]{2,1,0:T(8,128)(2,1)S(1)} copy-done((bf16[8,128,2048]{2,1,0:T(8,128)(2,1)S(1)}, bf16[8,128,2048]{2,1,0:T(8,128)(2,1)}, u32[]{:S(2)}) %copy-start.1) | copy-done | bytes 4194328
  113.7 3.4 %shard_map.81.refs_0_ = bf16[4,512,256]{2,1,0:T(8,128)(2,1)} custom-call(s32[1]{0:T(128)} %bitcast.ids, bf16[1024,2048]{1,0:T(8,128)(2,1)S(1)} %bitcast.13, bf16[128,256]{1,0:T(8,128)(2,1)S(1)} %get-tuple-element.33.refs_8_.refs_0_, bf16[128,256]{1,0:T(8,128)(2,1)S(1)} %collective-permute-done.7.refs_1_, ...), custom_call_target="tpu_custom_call" | custom-call | flops 1073741824 | bytes 5767168 | tf_op jit(solution)/shard_map/pallas_call | solution.py:155
  117.3 24.4 %all_to_all.26 = bf16[32,64,128]{2,1,0:T(8,128)(2,1)S(1)} all-to-all(bf16[32,64,128]{2,1,0:T(8,128)(2,1)S(1)} %get-tuple-element.43.refs_0_), channel_id=1, replica_groups=mesh['seq'=32,'dp'=8] {'seq'}, dimensions={0} | all-to-all | bytes 1048576 | tf_op jit(solution)/shard_map/all_to_all | solution.py:189
  141.6 4.1 %reduce-scatter.2.cloned.1.call-done = bf16[512,256]{1,0:T(8,128)(2,1)} async-done(((bf16[2048,256]{1,0:T(8,128)(2,1)}), bf16[512,256]{1,0:T(8,128)(2,1)}) %reduce-scatter.2.cloned.1.call-update) | async-done | bytes 262160 | tf_op jit(solution)/shard_map/reduce_scatter | solution.py:245
  145.7 6.6 %all-to-all-start.4 = ((bf16[8,64,256]{2,1,0:T(8,128)(2,1)}), bf16[8,64,256]{2,1,0:T(8,128)(2,1)S(1)}, u32[]{:S(2)}, u32[]{:S(2)}) async-start(bf16[8,64,256]{2,1,0:T(8,128)(2,1)} %bitcast.30), calls=%async_computation.5 | async-start | bytes 524288 | tf_op jit(solution)/shard_map/all_to_all | solution.py:189
  154.5 3.0 %shard_map.83 = (bf16[128,2048]{1,0:T(8,128)(2,1)}, bf16[2048,128]{1,0:T(8,128)(2,1)S(1)}) custom-call(s32[1]{0:T(128)} %bitcast.ids, bf16[128,2048]{1,0:T(8,128)(2,1)S(1)} %bitcast.27, bf16[128,2048]{1,0:T(8,128)(2,1)S(1)} %bitcast.16, bf16[128,2048]{1,0:T(8,128)(2,1)S(1)} %copy-done.11, bf16[2048,128]{1,0:T(8,128)(2,1)S(1)} %bitcast.22, ...), custom_call_target="tpu_custom_call" | custom-call | flops 201326592 | bytes 3145728 | tf_op jit(solution)/shard_map/pallas_call | solution.py:155
  157.5 1.4 shard_map.84
  158.9 3.6 %all-to-all-done.4.part_ref = bf16[8,64,256]{2,1,0:T(8,128)(2,1)S(1)} async-done(((bf16[8,64,256]{2,1,0:T(8,128)(2,1)}), bf16[8,64,256]{2,1,0:T(8,128)(2,1)S(1)}, u32[]{:S(2)}, u32[]{:S(2)}) %all-to-all-start.4) | async-done | bytes 262176 | tf_op jit(solution)/shard_map/all_to_all | solution.py:189
  162.5 15.4 %all-gather = bf16[512,256]{1,0:T(8,128)(2,1)S(1)} all-gather(bf16[64,256]{1,0:T(8,128)(2,1)S(1)} %shard_map.85), channel_id=2, replica_groups=mesh['seq'=32,'dp'=8] {'dp'}, dimensions={0}, use_global_device_ids=true | all-gather | bytes 294912 | tf_op jit(solution)/shard_map/all_gather | solution.py:254
  (56 shorter events, 18.5 us)
Async XLA Ops:
  7.2 61.6 %all-gather.3.cloned.1.call-start = ((), (), s32[]{:S(2)}) async-start(), calls=%async_computation.6 | async-start | bytes 4718592 | tf_op jit(solution)/shard_map/all_gather | solution.py:203
  60.7 22.1 %all-to-all-start.1 = ((bf16[32,64,128]{2,1,0:T(8,128)(2,1)}), bf16[32,64,128]{2,1,0:T(8,128)(2,1)S(1)}, u32[]{:S(2)}, u32[]{:S(2)}) async-start(bf16[32,64,128]{2,1,0:T(8,128)(2,1)} %shard_map.77.refs_0_), calls=%async_computation.1 | async-start | bytes 1048576 | tf_op jit(solution)/shard_map/all_to_all | solution.py:189
  68.8 2.2 %copy-start = (bf16[8,128,2048]{2,1,0:T(8,128)(2,1)S(1)}, bf16[8,128,2048]{2,1,0:T(8,128)(2,1)}, u32[]{:S(2)}) copy-start(bf16[8,128,2048]{2,1,0:T(8,128)(2,1)} %all-gather.3.cloned.1.call-done.x_ref) | copy-start | bytes 12582916
  71.0 11.8 %copy-start.3 = (bf16[1,128,2048]{2,1,0:T(8,128)(2,1)S(1)}, bf16[1,128,2048]{2,1,0:T(8,128)(2,1)}, u32[]{:S(2)}) copy-start(bf16[1,128,2048]{2,1,0:T(8,128)(2,1)} %param.8) | copy-start | bytes 1572868
  71.0 11.8 %copy-start.4 = (bf16[1,128,2048]{2,1,0:T(8,128)(2,1)S(1)}, bf16[1,128,2048]{2,1,0:T(8,128)(2,1)}, u32[]{:S(2)}) copy-start(bf16[1,128,2048]{2,1,0:T(8,128)(2,1)} %param.7) | copy-start | bytes 1572868
  73.0 6.3 %collective-permute-start = (bf16[128,256]{1,0:T(8,128)(2,1)S(1)}, bf16[128,256]{1,0:T(8,128)(2,1)S(1)}, u32[]{:S(2)}, u32[]{:S(2)}) collective-permute-start(bf16[128,256]{1,0:T(8,128)(2,1)S(1)} %get-tuple-element.26), channel_id=1, source_target_pairs={{0,1},{1,0},{2,3},{3,2},{4,5},{5,4},{6,7},{7,6},{8,9},{9,8},{10,11... | collective-permute-start | bytes 196616 | tf_op jit(solution)/shard_map/ppermute | solution.py:193
  74.3 7.5 %collective-permute-start.1 = (bf16[128,256]{1,0:T(8,128)(2,1)S(1)}, bf16[128,256]{1,0:T(8,128)(2,1)S(1)}, u32[]{:S(2)}, u32[]{:S(2)}) collective-permute-start(bf16[128,256]{1,0:T(8,128)(2,1)S(1)} %get-tuple-element.27), channel_id=1, source_target_pairs={{0,2},{1,3},{2,0},{3,1},{4,6},{5,7},{6,4},{7,5},{8,10},{9,11},{10,... | collective-permute-start | bytes 196616 | tf_op jit(solution)/shard_map/ppermute | solution.py:193
  75.5 9.3 %collective-permute-start.2 = (bf16[128,256]{1,0:T(8,128)(2,1)S(1)}, bf16[128,256]{1,0:T(8,128)(2,1)S(1)}, u32[]{:S(2)}, u32[]{:S(2)}) collective-permute-start(bf16[128,256]{1,0:T(8,128)(2,1)S(1)} %get-tuple-element.28), channel_id=1, source_target_pairs={{0,3},{1,2},{2,1},{3,0},{4,7},{5,6},{6,5},{7,4},{8,11},{9,10},{10,... | collective-permute-start | bytes 196616 | tf_op jit(solution)/shard_map/ppermute | solution.py:193
  76.0 8.8 %collective-permute-start.3 = (bf16[128,256]{1,0:T(8,128)(2,1)S(1)}, bf16[128,256]{1,0:T(8,128)(2,1)S(1)}, u32[]{:S(2)}, u32[]{:S(2)}) collective-permute-start(bf16[128,256]{1,0:T(8,128)(2,1)S(1)} %get-tuple-element.29), channel_id=1, source_target_pairs={{0,4},{1,5},{2,6},{3,7},{4,0},{5,1},{6,2},{7,3},{8,12},{9,13},{10,... | collective-permute-start | bytes 196616 | tf_op jit(solution)/shard_map/ppermute | solution.py:193
  78.8 6.1 %collective-permute-start.4 = (bf16[128,256]{1,0:T(8,128)(2,1)S(1)}, bf16[128,256]{1,0:T(8,128)(2,1)S(1)}, u32[]{:S(2)}, u32[]{:S(2)}) collective-permute-start(bf16[128,256]{1,0:T(8,128)(2,1)S(1)} %get-tuple-element.30), channel_id=1, source_target_pairs={{0,5},{1,4},{2,7},{3,6},{4,1},{5,0},{6,3},{7,2},{8,13},{9,12},{10,... | collective-permute-start | bytes 196616 | tf_op jit(solution)/shard_map/ppermute | solution.py:193
  79.3 6.9 %collective-permute-start.5 = (bf16[128,256]{1,0:T(8,128)(2,1)S(1)}, bf16[128,256]{1,0:T(8,128)(2,1)S(1)}, u32[]{:S(2)}, u32[]{:S(2)}) collective-permute-start(bf16[128,256]{1,0:T(8,128)(2,1)S(1)} %get-tuple-element.31), channel_id=1, source_target_pairs={{0,6},{1,7},{2,4},{3,5},{4,2},{5,3},{6,0},{7,1},{8,14},{9,15},{10,... | collective-permute-start | bytes 196616 | tf_op jit(solution)/shard_map/ppermute | solution.py:193
  81.8 5.7 %collective-permute-start.6 = (bf16[128,256]{1,0:T(8,128)(2,1)S(1)}, bf16[128,256]{1,0:T(8,128)(2,1)S(1)}, u32[]{:S(2)}, u32[]{:S(2)}) collective-permute-start(bf16[128,256]{1,0:T(8,128)(2,1)S(1)} %get-tuple-element.32), channel_id=1, source_target_pairs={{0,7},{1,6},{2,5},{3,4},{4,3},{5,2},{6,1},{7,0},{8,15},{9,14},{10,... | collective-permute-start | bytes 196616 | tf_op jit(solution)/shard_map/ppermute | solution.py:193
  89.5 27.7 %all-to-all-start.2 = ((bf16[32,64,128]{2,1,0:T(8,128)(2,1)}), bf16[32,64,128]{2,1,0:T(8,128)(2,1)S(1)}, u32[]{:S(2)}, u32[]{:S(2)}) async-start(bf16[32,64,128]{2,1,0:T(8,128)(2,1)} %bitcast.5), calls=%async_computation.2 | async-start | bytes 1048576 | tf_op jit(solution)/shard_map/all_to_all | solution.py:189
  99.0 46.8 %reduce-scatter.2.cloned.1.call-start = ((), (), s32[]{:S(2)}) async-start(), calls=%async_computation.7 | async-start | bytes 1310720 | tf_op jit(solution)/shard_map/reduce_scatter | solution.py:245
  99.0 5.8 %collective-permute-start.7 = (bf16[128,256]{1,0:T(8,128)(2,1)S(1)}, bf16[128,256]{1,0:T(8,128)(2,1)S(1)}, u32[]{:S(2)}, u32[]{:S(2)}) collective-permute-start(bf16[128,256]{1,0:T(8,128)(2,1)S(1)} %get-tuple-element.36), channel_id=1, source_target_pairs={{0,1},{1,0},{2,3},{3,2},{4,5},{5,4},{6,7},{7,6},{8,9},{9,8},{10,11... | collective-permute-start | bytes 196616 | tf_op jit(solution)/shard_map/ppermute | solution.py:193
  99.8 5.6 %collective-permute-start.8 = (bf16[128,256]{1,0:T(8,128)(2,1)S(1)}, bf16[128,256]{1,0:T(8,128)(2,1)S(1)}, u32[]{:S(2)}, u32[]{:S(2)}) collective-permute-start(bf16[128,256]{1,0:T(8,128)(2,1)S(1)} %get-tuple-element.37), channel_id=1, source_target_pairs={{0,2},{1,3},{2,0},{3,1},{4,6},{5,7},{6,4},{7,5},{8,10},{9,11},{10,... | collective-permute-start | bytes 196616 | tf_op jit(solution)/shard_map/ppermute | solution.py:193
  99.8 7.9 %collective-permute-start.9 = (bf16[128,256]{1,0:T(8,128)(2,1)S(1)}, bf16[128,256]{1,0:T(8,128)(2,1)S(1)}, u32[]{:S(2)}, u32[]{:S(2)}) collective-permute-start(bf16[128,256]{1,0:T(8,128)(2,1)S(1)} %get-tuple-element.38), channel_id=1, source_target_pairs={{0,3},{1,2},{2,1},{3,0},{4,7},{5,6},{6,5},{7,4},{8,11},{9,10},{10,... | collective-permute-start | bytes 196616 | tf_op jit(solution)/shard_map/ppermute | solution.py:193
  101.5 6.2 %collective-permute-start.10 = (bf16[128,256]{1,0:T(8,128)(2,1)S(1)}, bf16[128,256]{1,0:T(8,128)(2,1)S(1)}, u32[]{:S(2)}, u32[]{:S(2)}) collective-permute-start(bf16[128,256]{1,0:T(8,128)(2,1)S(1)} %get-tuple-element.39), channel_id=1, source_target_pairs={{0,4},{1,5},{2,6},{3,7},{4,0},{5,1},{6,2},{7,3},{8,12},{9,13},{10,... | collective-permute-start | bytes 196616 | tf_op jit(solution)/shard_map/ppermute | solution.py:193
  102.6 6.0 %collective-permute-start.11 = (bf16[128,256]{1,0:T(8,128)(2,1)S(1)}, bf16[128,256]{1,0:T(8,128)(2,1)S(1)}, u32[]{:S(2)}, u32[]{:S(2)}) collective-permute-start(bf16[128,256]{1,0:T(8,128)(2,1)S(1)} %get-tuple-element.40), channel_id=1, source_target_pairs={{0,5},{1,4},{2,7},{3,6},{4,1},{5,0},{6,3},{7,2},{8,13},{9,12},{10,... | collective-permute-start | bytes 196616 | tf_op jit(solution)/shard_map/ppermute | solution.py:193
  104.8 4.9 %collective-permute-start.12 = (bf16[128,256]{1,0:T(8,128)(2,1)S(1)}, bf16[128,256]{1,0:T(8,128)(2,1)S(1)}, u32[]{:S(2)}, u32[]{:S(2)}) collective-permute-start(bf16[128,256]{1,0:T(8,128)(2,1)S(1)} %get-tuple-element.41), channel_id=1, source_target_pairs={{0,6},{1,7},{2,4},{3,5},{4,2},{5,3},{6,0},{7,1},{8,14},{9,15},{10,... | collective-permute-start | bytes 196616 | tf_op jit(solution)/shard_map/ppermute | solution.py:193
  105.4 6.2 %collective-permute-start.13 = (bf16[128,256]{1,0:T(8,128)(2,1)S(1)}, bf16[128,256]{1,0:T(8,128)(2,1)S(1)}, u32[]{:S(2)}, u32[]{:S(2)}) collective-permute-start(bf16[128,256]{1,0:T(8,128)(2,1)S(1)} %get-tuple-element.42), channel_id=1, source_target_pairs={{0,7},{1,6},{2,5},{3,4},{4,3},{5,2},{6,1},{7,0},{8,15},{9,14},{10,... | collective-permute-start | bytes 196616 | tf_op jit(solution)/shard_map/ppermute | solution.py:193
  117.2 35.1 %copy-start.8 = (bf16[32,64,128]{2,1,0:T(8,128)(2,1)}, bf16[32,64,128]{2,1,0:T(8,128)(2,1)S(1)}, u32[]{:S(2)}) copy-start(bf16[32,64,128]{2,1,0:T(8,128)(2,1)S(1)} %get-tuple-element.43.refs_0_) | copy-start | bytes 1572868
  117.3 35.1 %copy-start.7 = (bf16[1,128,2048]{2,1,0:T(8,128)(2,1)S(1)}, bf16[1,128,2048]{2,1,0:T(8,128)(2,1)}, u32[]{:S(2)}) copy-start(bf16[1,128,2048]{2,1,0:T(8,128)(2,1)} %param.6) | copy-start | bytes 1572868
  145.7 16.7 %all-to-all-start.4 = ((bf16[8,64,256]{2,1,0:T(8,128)(2,1)}), bf16[8,64,256]{2,1,0:T(8,128)(2,1)S(1)}, u32[]{:S(2)}, u32[]{:S(2)}) async-start(bf16[8,64,256]{2,1,0:T(8,128)(2,1)} %bitcast.30), calls=%async_computation.5 | async-start | bytes 524288 | tf_op jit(solution)/shard_map/all_to_all | solution.py:189
  (8 other events, 9.1 us)
Sparse Core Ops, SparseCore 0:
  9.9 38.8 all-gather.2
  117.4 28.2 reduce-scatter.1
